TPU v7x, 32 devices: a whole 2x2x4 slice. The times are simulated.
32 devices in a mesh: spot: 16 (over z, x, core), grp: 2 (over y).
Axes of the slice: x: 2, y: 2, z: 4, core: 2. Of those that a mesh axis runs over, the one named last changes fastest.
Arguments:
- map_logits: bfloat16 [16384, 4096], P(None, ('spot', 'grp')), may hold values from -8 to 8
- single_cell: bfloat16 [16384, 2048], P(('spot', 'grp')), may hold values from -1.671875 to 1.71875
- spatial: bfloat16 [4096, 2048], P(('spot', 'grp')), may hold values from 0 to 2
- slide_ids: int32 [4096], P(('spot', 'grp')), may hold values from 0 to 2
- spot_mask: int32 [4096], P(('spot', 'grp')), may hold values 0 or 1
- cell_prior: float32 [16384], replicated, may hold values from 0.2 to 5
- gene_order: int32 [4], replicated, may hold values from 0 to 3, each once
Outputs:
- loss_terms: float32 [3], replicated
- grad_map: float32 [16384, 4096], P(None, ('spot', 'grp'))
- grad_single: float32 [16384, 2048], P(('spot', 'grp'))
All inputs are finite; a program needn't handle non-finite values. No bound on the sum of `spot_mask` on one device may be relied on, other than what follows from the above.
Results may differ from a plain program's by a relative error of at most 0.0032.
Values may be sent and summed in bfloat16 or wider, within the bound.
A program may use at most 384 MiB of HBM per device.

v0:
```python
import jax
import jax.numpy as jnp
from jax import lax
from jax.sharding import PartitionSpec as P

SLIDES = 3


STABILITY_FLOOR = 1e-06
FULL_ACCURACY = lax.Precision.HIGHEST


def body(map_logits, single_cell, spatial, slide_ids, spot_mask, cell_prior, gene_order):
    cells = map_logits.shape[0]
    spots_here = map_logits.shape[1]
    genes = spatial.shape[1]
    blocks = gene_order.shape[0]
    width = genes // blocks
    scores = map_logits.astype(jnp.float32)
    raised = jnp.exp(scores - jnp.max(scores, axis=0, keepdims=True))
    shares = raised / jnp.sum(raised, axis=0, keepdims=True)
    shares_low = shares.astype(jnp.bfloat16)
    weight_factor = spot_mask.astype(jnp.float32)
    group_members = (slide_ids[:, None] == jnp.arange(SLIDES, dtype=jnp.int32)[None, :]).astype(
        jnp.float32
    ) * weight_factor[:, None]
    local_mass = jnp.einsum("sk,cs->kc", group_members, shares, precision=FULL_ACCURACY)
    local_tally = jnp.sum(group_members, axis=0)
    measured_expression = spatial.astype(jnp.float32)
    predicted_parts = []
    statistic_pieces = []
    for block_index in range(blocks):
        local_block = lax.dynamic_slice_in_dim(
            single_cell, gene_order[block_index] * width, width, 1
        )
        predicted_expression = lax.dot_general(
            shares_low,
            lax.all_gather(local_block, ("spot", "grp"), axis=0, tiled=True),
            (((0,), (0,)), ((), ())),
            preferred_element_type=jnp.float32,
        )
        observed = measured_expression[:, block_index * width : (block_index + 1) * width]
        block_stats = (
            jnp.einsum(
                "sk,sg->kg", group_members, predicted_expression * observed, precision=FULL_ACCURACY
            ),
            jnp.einsum(
                "sk,sg->kg",
                group_members,
                predicted_expression * predicted_expression,
                precision=FULL_ACCURACY,
            ),
            jnp.einsum("sk,sg->kg", group_members, observed * observed, precision=FULL_ACCURACY),
        )
        block_stats = lax.psum((block_stats[0], block_stats[1], block_stats[2]), ("spot", "grp"))
        statistic_pieces.append(block_stats)
        predicted_parts.append(predicted_expression)
    predicted_expression = jnp.concatenate(predicted_parts, axis=1)
    gene_inner_product = jnp.concatenate([part[0] for part in statistic_pieces], axis=1)
    gene_predicted_norm = jnp.concatenate([part[1] for part in statistic_pieces], axis=1)
    gene_measured_norm = jnp.concatenate([part[2] for part in statistic_pieces], axis=1)
    inverse_predicted_norm = lax.rsqrt(
        jnp.sum(predicted_expression * predicted_expression, axis=1) + STABILITY_FLOOR
    )
    inverse_measured_norm = lax.rsqrt(
        jnp.sum(measured_expression * measured_expression, axis=1) + STABILITY_FLOOR
    )
    spot_cosine_score = (
        jnp.sum(predicted_expression * measured_expression, axis=1)
        * inverse_predicted_norm
        * inverse_measured_norm
    )
    local_spot = jnp.sum(weight_factor * spot_cosine_score)
    mass, tally, spot_total = lax.psum((local_mass, local_tally, local_spot), ("spot", "grp"))
    tally = jnp.maximum(tally, 1.0)
    total = jnp.sum(tally)
    inv_gpred = lax.rsqrt(gene_predicted_norm + STABILITY_FLOOR)
    inverse_gene_measured_norm = lax.rsqrt(gene_measured_norm + STABILITY_FLOOR)
    gene_cosine_score = gene_inner_product * inv_gpred * inverse_gene_measured_norm
    gene_total = jnp.sum(tally / genes * jnp.sum(gene_cosine_score, axis=1))
    prior = cell_prior / jnp.sum(cell_prior)
    quota = mass / tally[:, None]
    diverge = jnp.sum(prior[None, :] * (jnp.log(prior)[None, :] - jnp.log(quota)), axis=1)
    density_total = jnp.sum(tally * diverge)
    loss_terms = jnp.stack([spot_total / total, gene_total / total, density_total / total])
    factor_gene = (tally / genes)[:, None]
    direct = jnp.dot(
        group_members, factor_gene * inv_gpred * inverse_gene_measured_norm, precision=FULL_ACCURACY
    )
    damping = jnp.dot(
        group_members,
        factor_gene * gene_cosine_score * inv_gpred * inv_gpred,
        precision=FULL_ACCURACY,
    )
    grad_pred = (
        -(weight_factor * inverse_predicted_norm * inverse_measured_norm)[:, None]
        * measured_expression
        + (weight_factor * spot_cosine_score * inverse_predicted_norm * inverse_predicted_norm)[
            :, None
        ]
        * predicted_expression
        - direct * measured_expression
        + damping * predicted_expression
    )
    grad_low_pred = grad_pred.astype(jnp.bfloat16)
    back_low = jnp.zeros((cells, spots_here), jnp.float32)
    for block_index in range(blocks):
        grad_block = grad_low_pred[:, block_index * width : (block_index + 1) * width]
        local_block = lax.dynamic_slice_in_dim(
            single_cell, gene_order[block_index] * width, width, 1
        )

        def cell_terms(portion, offset, grad_block=grad_block):
            return lax.dot_general(
                portion, grad_block, (((1,), (1,)), ((), ())), preferred_element_type=jnp.float32
            )

        back_low = back_low + cell_terms(
            lax.all_gather(local_block, ("spot", "grp"), axis=0, tiled=True), jnp.int32(0)
        )
    ratio = prior[None, :] / quota
    grad_shares = back_low - jnp.einsum("kc,sk->cs", ratio, group_members, precision=FULL_ACCURACY)
    grad_map = (
        shares * (grad_shares - jnp.sum(shares * grad_shares, axis=0, keepdims=True)) * float(cells)
    )
    inverse = jnp.sum(
        jnp.arange(blocks, dtype=jnp.int32)[:, None]
        * (gene_order[:, None] == jnp.arange(blocks, dtype=jnp.int32)[None, :]).astype(jnp.int32),
        axis=0,
    )
    reordered = jnp.take(grad_low_pred.reshape(spots_here, blocks, width), inverse, axis=1).reshape(
        spots_here, genes
    )
    grad_single = (
        lax.psum_scatter(
            jnp.dot(shares_low, reordered, preferred_element_type=jnp.float32),
            ("spot", "grp"),
            scatter_dimension=0,
            tiled=True,
        )
        * float(cells) ** 0.5
    )
    return (loss_terms, grad_map, grad_single)


def solution(mesh):
    in_specs = (
        P(None, ("spot", "grp")),
        P(("spot", "grp"), None),
        P(("spot", "grp"), None),
        P(("spot", "grp")),
        P(("spot", "grp")),
        P(),
        P(),
    )
    out_specs = (P(), P(None, ("spot", "grp")), P(("spot", "grp"), None))
    return jax.shard_map(body, mesh=mesh, in_specs=in_specs, out_specs=out_specs, check_vma=False)
```

profile of v0, /device:TPU:9, one launch (start us, length us, event | category | flops | bytes accessed | tf_op | source)
XLA Modules:
  0.0 3465.3 jit_solution(17316947151909112148)
XLA Ops:
  7.2 0.0 all-gather.9.cloned.1.call-start
  7.2 1.5 fusion.155
  11.3 2.9 constant_dynamic-slice_fusion.3
  14.2 0.0 all-gather.9.cloned.1.call-update
  14.3 0.0 all-gather.11.cloned.1.call-start
  14.3 0.7 all-gather.11.cloned.1.call-update
  15.0 0.0 all-gather.7.cloned.1.call-start
  15.1 0.7 all-gather.7.cloned.1.call-update
  15.8 0.0 all-gather.5.cloned.1.call-start
  15.8 0.5 all-gather.5.cloned.1.call-update
  16.3 0.0 all-reduce.5.cloned.1.call-start
  16.4 0.7 convert_element_type.17
  17.0 3.8 reduce_max.14
  20.8 3.8 fusion.1
  24.7 10.1 fusion.57
  34.7 0.5 reduce-scatter.5.cloned.1.call-start
  35.3 0.1 select_reduce_fusion.1
  35.4 0.1 select_reduce_fusion
  35.5 0.1 convert_element_type.20
  35.6 0.3 fusion.13
  35.9 0.3 fusion.11
  36.1 0.3 fusion.9
  36.4 0.3 fusion.7
  36.6 0.1 broadcast_bitcast_fusion
  36.7 0.6 reduce_sum.137
  37.3 0.7 fusion.152
  38.0 92.1 %all-gather.9.cloned.1.call-done = bf16[16384,512]{1,0:T(8,128)(2,1)} async-done(((bf16[512,512]{1,0:T(8,128)(2,1)}), bf16[16384,512]{1,0:T(8,128)(2,1)}) %all-gather.9.cloned.1.call-update) | async-done | bytes 16777232 | tf_op jit(solution)/shard_map/all_gather | solution.py:38
  130.1 9.9 fusion.146
  140.1 0.3 fusion.17
  140.3 0.2 fusion.25
  140.6 105.5 %all-gather.11.cloned.1.call-done = bf16[16384,512]{1,0:T(8,128)(2,1)} async-done(((bf16[512,512]{1,0:T(8,128)(2,1)}), bf16[16384,512]{1,0:T(8,128)(2,1)}) %all-gather.11.cloned.1.call-update) | async-done | bytes 16777232 | tf_op jit(solution)/shard_map/all_gather | solution.py:38
  246.1 9.9 fusion.144
  256.0 0.3 fusion.15
  256.3 0.3 fusion.23
  256.5 106.1 %all-gather.7.cloned.1.call-done = bf16[16384,512]{1,0:T(8,128)(2,1)} async-done(((bf16[512,512]{1,0:T(8,128)(2,1)}), bf16[16384,512]{1,0:T(8,128)(2,1)}) %all-gather.7.cloned.1.call-update) | async-done | bytes 16777232 | tf_op jit(solution)/shard_map/all_gather | solution.py:38
  362.6 9.9 fusion.148
  372.6 0.3 fusion.19
  372.8 0.2 fusion.27
  373.1 106.0 %all-gather.5.cloned.1.call-done = bf16[16384,512]{1,0:T(8,128)(2,1)} async-done(((bf16[512,512]{1,0:T(8,128)(2,1)}), bf16[16384,512]{1,0:T(8,128)(2,1)}) %all-gather.5.cloned.1.call-update) | async-done | bytes 16777232 | tf_op jit(solution)/shard_map/all_gather | solution.py:38
  479.0 9.9 fusion.150
  489.0 0.4 fusion.29
  489.4 0.3 multiply_reduce_fusion.2
  489.7 0.3 fusion.21
  490.0 0.6 reduce_sum.132
  490.6 40.3 %all-reduce.6 = (f32[3,512]{1,0:T(4,128)S(1)}, f32[3,512]{1,0:T(4,128)S(1)}, f32[3,512]{1,0:T(4,128)S(1)}, f32[3,512]{1,0:T(4,128)S(1)}, f32[3,512]{1,0:T(4,128)...) all-reduce(f32[3,512]{1,0:T(4,128)S(1)} %fusion.23, ...), channel_id=1, replica_groups=mesh['spot'=16,'grp'=2] {'spot','grp'}, use_global_device_ids=true, to_apply=%region_13.0 | all-reduce | flops 18436 | bytes 147488 | tf_op jit(solution)/shard_map/psum | solution.py:55
  531.0 0.1 fusion.153
  531.1 75.2 %all-reduce.5.cloned.1.call-done = f32[3,16384]{1,0:T(4,128)} async-done(((f32[3,16384]{1,0:T(4,128)}), f32[3,16384]{1,0:T(4,128)}) %all-reduce.5.cloned.1.call-update) | async-done | bytes 196624 | tf_op jit(solution)/shard_map/psum | solution.py:74
  606.3 1.3 multiply_reduce_fusion.4
  607.6 0.7 multiply_reduce_fusion.6
  608.3 1.2 fusion.3
  609.5 1.0 fusion.4
  610.6 0.6 gather_fusion
  611.1 0.3 copy.16
  611.4 0.3 bitcast_select_fusion
  611.8 45.4 %fusion.142 = f32[16384,2048]{1,0:T(8,128)} fusion(bf16[128,2048]{0,1:T(8,128)(2,1)S(1)} %bitcast_select_fusion, f32[128]{0:T(128)S(1)} %fusion.1, f32[128]{0:T(128)S(1)} %reduce_max.15, bf16[16384,128]{1,0:T(8,128)(2,1)} %param.7), kind=kOutput, calls=%fused_computation.184 | convolution fusion | flops 8598323200 | bytes 138937344 | tf_op jit(solution)/shard_map/dot_general | solution.py:136
  661.3 0.6 pad_maximum_fusion.1
  661.9 9.1 fusion.42
  671.0 14.2 convolution_add_fusion.2
  685.2 12.8 convolution_add_fusion.1
  698.0 14.7 convolution_add_fusion
  712.7 16.4 multiply_reduce_fusion
  729.0 4.5 multiply_multiply_fusion
  733.6 2719.6 %reduce-scatter.5.cloned.1.call-done = f32[512,2048]{1,0:T(8,128)} async-done(((f32[16384,2048]{1,0:T(8,128)}), f32[512,2048]{1,0:T(8,128)}) %reduce-scatter.5.cloned.1.call-update) | async-done | bytes 4194320
  3453.2 4.8 broadcast_multiply_fusion
  (24 shorter events, 0.2 us)
Async XLA Ops:
  7.2 17.5 copy-start.4
  7.2 122.9 %all-gather.9.cloned.1.call-start = ((), (), s32[]{:S(2)}) async-start(), calls=%async_computation.3 | async-start | bytes 17301504 | tf_op jit(solution)/shard_map/all_gather | solution.py:38
  14.3 231.8 %all-gather.11.cloned.1.call-start = ((), (), s32[]{:S(2)}) async-start(), calls=%async_computation.4 | async-start | bytes 17301504 | tf_op jit(solution)/shard_map/all_gather | solution.py:38
  15.0 347.6 %all-gather.7.cloned.1.call-start = ((), (), s32[]{:S(2)}) async-start(), calls=%async_computation.2 | async-start | bytes 17301504 | tf_op jit(solution)/shard_map/all_gather | solution.py:38
  15.8 463.3 %all-gather.5.cloned.1.call-start = ((), (), s32[]{:S(2)}) async-start(), calls=%async_computation.1 | async-start | bytes 17301504 | tf_op jit(solution)/shard_map/all_gather | solution.py:38
  16.3 590.0 %all-reduce.5.cloned.1.call-start = ((), (), s32[]{:S(2)}) async-start(), calls=%async_computation.5 | async-start | bytes 524288 | tf_op jit(solution)/shard_map/psum | solution.py:74
  24.6 10.6 copy-start.5
  24.6 10.9 copy-start.1
  24.6 12.1 copy-start.2
  34.7 3418.5 %reduce-scatter.5.cloned.1.call-start = ((), (), s32[]{:S(2)}) async-start(), calls=%async_computation.6 | async-start | bytes 138412032
  373.1 116.9 %copy-start.6 = (s32[128]{0:T(128)S(1)}, s32[128]{0:T(128)}, u32[]{:S(2)}) copy-start(s32[128]{0:T(128)} %param.11) | copy-start | bytes 1540
  698.0 14.7 copy-start
  698.0 14.7 copy-start.3
Sparse Core Ops, SparseCore 0:
  14.4 115.6 all-gather.8
  133.0 113.0 all-gather.10
  249.6 113.0 all-gather.6
  365.9 113.0 all-gather.4
  484.4 121.8 all-reduce.4
  657.4 2795.8 reduce-scatter.4
where the time goes:
time: 3470 us
  waiting for transfers between devices  3210 us (93%)
  matrix products  168 us (5%)
  blocking collectives  40.3 us (1%)
    unnamed x7, waiting for transfers between devices  2720 us
    all_gather x4, waiting for transfers between devices, body(): lax.all_gather(local_block, ('spot', 'grp'), axis=0, tiled=True)  410 us
    psum x1, waiting for transfers between devices, body(): lax.psum((local_mass, local_tally, local_spot), ('spot', 'grp'))  75.2 us
  transfers between devices with their start and end apart: 6, of which 6 were waited for; matrix products, arithmetic and copies ran while one was open for 4% of the time, Pallas kernels for 0%

commit v1 on v0

v1 whole, which is shorter than its diff:
```python
import functools

import jax
import jax.numpy as jnp
from jax import lax
from jax.experimental import pallas as pl
from jax.experimental.pallas import tpu as pltpu
from jax.sharding import Mesh, PartitionSpec as P

SLIDES = 3
FLOOR = 1e-06
F32 = jnp.float32
BF16 = jnp.bfloat16
AXES = ("z", "x", "c", "y")
MESH_ID = pl.DeviceIdType.MESH


def flip(value, mask):
    bit = 1
    while bit <= mask:
        if mask & bit:
            value = value + (1 - 2 * ((value // bit) % 2)) * bit
        bit *= 2
    return value


class Sizes:
    def __init__(self, mesh, cells, genes, spots, blocks):
        n = mesh.shape["spot"] // 2
        zs = 1
        while zs * zs * 4 <= 2 * n:
            zs *= 2
        self.Z, self.X, self.Y = zs, n // zs, mesh.shape["grp"]
        assert self.Y == 2 and self.Z * self.X == n and self.Z >= 2
        self.LV = self.Z.bit_length() - 1
        self.A = 2 * self.Z
        self.Q = self.X * self.Y
        self.CELLS, self.G, self.S, self.NB = cells, genes, spots, blocks
        self.R = cells // (self.A * self.Q)
        self.H = self.R // 2
        self.YR = self.Y * self.R
        self.NC = self.X * self.YR
        self.GA = genes // self.A
        self.RC = min(256, self.YR)
        self.NN = min(512, genes)


def kernel(k, logits, logits_flat, own_cells, spatial, ids, mask, cell_prior, order,
           out_map, out_single, out_loss,
           lbuf, cells, slow, slow_t, ybuf, info, info2,
           pacc, p1, psib, rs_out, rs_in, pred, meas,
           gp, gsend, grecv,
           mass_out, mass_in, ratio_hl, mext, dpart, din,
           stat, s1, ubuf, s2, wall,
           loc_sem, lg_s, lg_r, cl_s, cl_r, in_s, in_r, ps_s, ps_r, rs_s, rs_r, ms_s, ms_r,
           d_s, d_r, s1_s, s1_r, s2_s, s2_r, s3_s, s3_r, gz_s, gz_r, gc_s, gc_r, i2_s, i2_r,
           y_s, y_r, gs_s, gs_r):
    Z, X, Y, A, Q, S, G, R, H = k.Z, k.X, k.Y, k.A, k.Q, k.S, k.G, k.R, k.H
    YR, NC, GA, RC, NN = k.YR, k.NC, k.GA, k.RC, k.NN
    z, x, c, y = [lax.axis_index(a) for a in AXES]
    yo = 1 - y

    def group(m, e):
        return (flip(z, m), x, flip(c, e), y)

    def plane(dx, dy):
        return (z, lax.rem(x + dx, X), c, flip(y, dy))

    def remote(src, dst, send, recv, where):
        return pltpu.make_async_remote_copy(
            src_ref=src, dst_ref=dst, send_sem=send, recv_sem=recv,
            device_id=where, device_id_type=MESH_ID)

    groups = [(m, e) for m in range(Z) for e in range(2) if (m, e) != (0, 0)]
    planes = [(dx, dy) for dx in range(X) for dy in range(Y) if (dx, dy) != (0, 0)]
    me = z * 2 + c
    pending = []

    cp_flat = pltpu.make_async_copy(logits_flat, ybuf, loc_sem.at[0])
    cp_flat.start()
    cp_own = pltpu.make_async_copy(logits.at[z, :, c], lbuf.at[0, 0], loc_sem.at[1])
    cp_own.start()
    cp_cells = pltpu.make_async_copy(
        own_cells, cells.at[pl.ds(pl.multiple_of((x * Y + y) * R, R), R)], loc_sem.at[2])
    cp_cells.start()
    barrier = pltpu.get_barrier_semaphore()
    for m, e in groups:
        pl.semaphore_signal(barrier, inc=1, device_id=group(m, e), device_id_type=MESH_ID)
    for dx, dy in planes:
        pl.semaphore_signal(barrier, inc=1, device_id=plane(dx, dy), device_id_type=MESH_ID)
    pl.semaphore_wait(barrier, len(groups) + len(planes))

    def rows(bx, by, half):
        return cells.at[pl.ds(pl.multiple_of(((bx * Y + by) * 2 + half) * H, H), H)]

    XN = X - 1

    def cell_copy(slot, src, bx, by, half, where):
        return remote(src, rows(bx, by, half), cl_s.at[slot], cl_r.at[slot], where)

    own_half = [own_cells.at[pl.ds(0, H)], own_cells.at[pl.ds(H, H)]]
    x_first = [cell_copy(d, own_half[0], x, y, 0, plane(d + 1, 0)) for d in range(XN)]
    x_last = [cell_copy(XN + d, own_half[1], x, y, 1, plane(d + 1, 0)) for d in range(XN)]
    y_first = cell_copy(2 * XN, own_half[1], x, y, 1, plane(0, 1))
    y_last = cell_copy(2 * XN + 1, own_half[0], x, y, 0, plane(0, 1))
    for cp in x_first + [y_first]:
        cp.start()

    lg = {}

    def send_logits(m, e):
        cp = remote(logits.at[flip(z, m), :, flip(c, e)], lbuf.at[m, e],
                    lg_s.at[m, e], lg_r.at[m, e], group(m, e))
        cp.start()
        lg[m, e] = cp
        pending.append(cp)

    high = Z // 2
    far = [m for m in range(Z) if m & high and m != high]
    near = [m for m in range(1, Z) if not m & high]
    for m in far + near + [high]:
        for e in range(2):
            send_logits(m, e)
    send_logits(0, 1)
    for cp in x_last + [y_last]:
        cp.start()
    pending.extend(x_first + x_last + [y_first, y_last])

    cp_flat.wait()

    def add_exp(i, acc):
        e = jnp.exp(ybuf[i].astype(F32))
        return acc + jnp.sum(e.reshape(YR // 8, 8, S), axis=0)

    acc = lax.fori_loop(0, A * X, add_exp, jnp.zeros((8, S), F32))
    inv_sum = 1.0 / jnp.sum(acc, axis=0, keepdims=True)
    idr = ids[...]
    maskf = mask[...].astype(F32)
    mrow = [jnp.where(idr == s, maskf, 0.0) for s in range(SLIDES)]
    info[0, 0] = jnp.concatenate([inv_sum] + mrow + [jnp.zeros((8 - 1 - SLIDES, S), F32)], axis=0)
    inf = {}
    for m, e in groups:
        inf[m, e] = remote(info.at[0, 0], info.at[m, e], in_s.at[m, e], in_r.at[m, e], group(m, e))
        inf[m, e].start()
        pending.append(inf[m, e])

    W = G // k.NB
    for b in range(k.NB):
        v = jnp.zeros((S, W), F32)
        for j in range(k.NB):
            here = (order[0:1, j:j + 1] == b).astype(F32)
            v = v + here * spatial[:, j * W:(j + 1) * W].astype(F32)
        meas[:, b * W:(b + 1) * W] = v.astype(BF16)
    mcols = jnp.concatenate(mrow + [maskf] + [jnp.zeros((8 - 1 - SLIDES, S), F32)], axis=0).T
    mcol = [mcols[:, s:s + 1] for s in range(SLIDES)]
    wcol = mcols[:, SLIDES:SLIDES + 1]
    meas_sq = jnp.zeros((S, 1), F32)
    for j in range(A):
        v = meas[:, j * GA:(j + 1) * GA].astype(F32)
        v = v * v
        meas_sq = meas_sq + jnp.sum(v, axis=1, keepdims=True)
        for s in range(SLIDES):
            stat[j, 6 + s:7 + s, :] = jnp.sum(mcol[s] * v, axis=0, keepdims=True)
    inv_meas = lax.rsqrt(meas_sq + FLOOR)

    fwd_a, fwd_b = [], []
    for d in range(XN):
        bx = lax.rem(x - (d + 1) + X, X)
        cell_copy(d, own_half[0], bx, y, 0, plane(d + 1, 0)).wait_recv()
        cp = cell_copy(2 * XN + 2 + d, rows(bx, y, 0), bx, y, 0, plane(0, 1))
        cp.start()
        fwd_a.append(cp)
    y_first.wait_recv()
    for d in range(XN):
        cp = cell_copy(3 * XN + 2 + d, rows(x, yo, 1), x, yo, 1, plane(d + 1, 0))
        cp.start()
        fwd_b.append(cp)
    pending.extend(fwd_a + fwd_b)

    cp_own.wait()
    cp_cells.wait()

    def shares_of(m, e, i):
        per = YR // RC
        l = lbuf[m, e, i // per, pl.ds(pl.multiple_of(lax.rem(i, per) * RC, RC), RC), :]
        return jnp.exp(l.astype(F32)) * info[m, e, 0:1, :]

    def make_shares(m):
        for e in range(2):
            if (m, e) != (0, 0):
                inf[m, e].wait_recv()
                lg[m, e].wait_recv()
        for e in range(2):
            lane = (m * 2 + e) * S

            def step(i, _):
                sh = shares_of(m, e, i)
                r0 = pl.multiple_of(i * RC, RC)
                slow[pl.ds(r0, RC), lane:lane + S] = sh.astype(BF16)
                slow_t[e * S:(e + 1) * S, pl.ds(r0, RC)] = sh.T.astype(BF16)
                return 0

            lax.fori_loop(0, NC // RC, step, 0)

    def predict(m):
        def step(i, _):
            lanes = pl.ds(pl.multiple_of(i * NN, NN), NN)
            r = jnp.dot(slow_t[...], cells[:, lanes], preferred_element_type=F32)
            pacc[m, :, lanes] = r[:S]
            p1[m, :, lanes] = r[S:].astype(BF16)
            return 0

        lax.fori_loop(0, G // NN, step, 0)
        cp = remote(p1.at[m], psib.at[m], ps_s.at[m], ps_r.at[m], group(0, 1))
        cp.start()
        pending.append(cp)
        return cp

    ps = {}
    first = True
    for m in far + near + [0, high] if Z > 2 else [0, high]:
        make_shares(m)
        if first:
            for cp in x_last + [y_last] + fwd_a + fwd_b:
                cp.wait_recv()
            first = False
        ps[m] = predict(m)

    rs = {}

    def level_slot(b, m):
        return sum(Z >> (j + 1) for j in range(b)) + (m >> (b + 1))

    def piece_sum(m, b):
        cps = [rs[j, m] for j in range(b)]
        ps[m].wait_recv()
        for cp in cps:
            cp.wait_recv()

        def total(lanes):
            t = pacc[m, :, lanes] + psib[m, :, lanes].astype(F32)
            for j in range(b):
                t = t + rs_in[level_slot(j, m), :, lanes].astype(F32)
            return t
        return total

    for b in range(k.LV):
        step_m = 1 << b
        ms = [m for m in range(step_m, Z, 2 * step_m)]
        for m in reversed(ms):
            total = piece_sum(m, b)
            slot = level_slot(b, m ^ step_m)
            rs_out[slot] = total(slice(0, G)).astype(BF16)
            cp = remote(rs_out.at[slot], rs_in.at[slot], rs_s.at[slot], rs_r.at[slot],
                        group(step_m, 0))
            cp.start()
            rs[b, m ^ step_m] = cp
            pending.append(cp)

    mem_rows = jnp.concatenate(
        [info[m, e, 1:1 + SLIDES, :] for m in range(Z) for e in range(2)], axis=1)
    mem16 = jnp.concatenate([mem_rows, jnp.zeros((16 - SLIDES, A * S), F32)], axis=0).astype(BF16)
    part = lax.dot_general(mem16, slow[...], (((1,), (1,)), ((), ())), preferred_element_type=F32)
    col_tally = jnp.sum(mem_rows, axis=1, keepdims=True)
    mass_out[...] = jnp.concatenate(
        [part[:SLIDES], jnp.broadcast_to(col_tally, (SLIDES, NC)), jnp.zeros((2, NC), F32)], axis=0)
    mcp = []
    for i, (dx, dy) in enumerate(planes):
        cp = remote(mass_out, mass_in.at[i], ms_s.at[i], ms_r.at[i], plane(dx, dy))
        cp.start()
        mcp.append(cp)
    pending.extend(mcp)
    for cp in mcp:
        cp.wait_recv()
    msum = mass_out[...]
    for i in range(Q - 1):
        msum = msum + mass_in[i]
    mass = msum[:SLIDES]
    tally = jnp.maximum(msum[SLIDES:2 * SLIDES, 0:1], 1.0)
    quota = mass / tally
    prior_sum = jnp.sum(jnp.sum(cell_prior[...], axis=0, keepdims=True), axis=1, keepdims=True)
    prior = jnp.concatenate(
        [cell_prior[pl.ds((z * X + bx) * 2 + c, 1), :] for bx in range(X)], axis=1) / prior_sum
    kl = jnp.sum(prior * (jnp.log(prior) - jnp.log(quota)), axis=1, keepdims=True)
    rat = prior / quota
    rat_hi = rat.astype(BF16)
    rat_lo = (rat - rat_hi.astype(F32)).astype(BF16)
    ratio_hl[...] = jnp.concatenate(
        [rat_hi, rat_lo, jnp.zeros((16 - 2 * SLIDES, NC), BF16)], axis=0)
    dd = jnp.dot(ratio_hl[...], slow[...], preferred_element_type=F32)
    dd = dd[:SLIDES] + dd[SLIDES:2 * SLIDES]
    dsum = jnp.sum(dd * mem_rows, axis=0, keepdims=True)
    mext[...] = jnp.concatenate(
        [mem_rows, mem_rows, jnp.zeros((16 - 2 * SLIDES, A * S), F32)], axis=0).astype(BF16)
    dcp = {}
    for m in range(Z):
        for e in range(2):
            lane = (m * 2 + e) * S
            dpart[m, e] = jnp.broadcast_to(dsum[:, lane:lane + S], (8, S))
    for m, e in groups:
        cp = remote(dpart.at[m, e], din.at[m, e], d_s.at[m, e], d_r.at[m, e], group(m, e))
        cp.start()
        dcp[m, e] = cp
        pending.append(cp)

    total = piece_sum(0, k.LV)
    pred_sq = jnp.zeros((S, 1), F32)
    pred_meas = jnp.zeros((S, 1), F32)
    lane_id = lax.broadcasted_iota(jnp.int32, (1, GA), 1)
    for j in range(A):
        lanes = slice(j * GA, (j + 1) * GA)
        p = total(lanes)
        pred[:, lanes] = p
        q = meas[:, lanes].astype(F32)
        pq, pp = p * q, p * p
        pred_sq = pred_sq + jnp.sum(pp, axis=1, keepdims=True)
        pred_meas = pred_meas + jnp.sum(pq, axis=1, keepdims=True)
        for s in range(SLIDES):
            stat[j, s:s + 1, :] = jnp.sum(mcol[s] * pq, axis=0, keepdims=True)
            stat[j, 3 + s:4 + s, :] = jnp.sum(mcol[s] * pp, axis=0, keepdims=True)
    inv_pred = lax.rsqrt(pred_sq + FLOOR)
    spot_cos = pred_meas * inv_pred * inv_meas
    spot_sum = jnp.sum(wcol * spot_cos, axis=0, keepdims=True)
    scal = jnp.where(lane_id == 0, spot_sum, 0.0)
    for s in range(SLIDES):
        scal = scal + jnp.where(lane_id == 1 + s, kl[s:s + 1] * (1.0 / Q), 0.0)
    for j in range(A):
        stat[j, 9:16, :] = jnp.concatenate([scal, jnp.zeros((6, GA), F32)], axis=0)

    cps = {}
    for m, e in groups:
        cp = remote(stat.at[flip(z, m) * 2 + flip(c, e)], s1.at[m, e],
                    s1_s.at[m, e], s1_r.at[m, e], group(m, e))
        cp.start()
        cps[m, e] = cp
        pending.append(cp)
    u = stat[me]
    for m, e in groups:
        cps[m, e].wait_recv()
        u = u + s1[m, e]
    ubuf[...] = u
    cps = []
    for i, (dx, dy) in enumerate(planes):
        cp = remote(ubuf, s2.at[i], s2_s.at[i], s2_r.at[i], plane(dx, dy))
        cp.start()
        cps.append(cp)
        pending.append(cp)
    for i, cp in enumerate(cps):
        cp.wait_recv()
        u = u + s2[i]
    share = tally * (1.0 / G)
    a = lax.rsqrt(u[3:6] + FLOOR)
    b = lax.rsqrt(u[6:9] + FLOOR)
    gcos = u[0:3] * a * b
    wall[me] = jnp.concatenate(
        [share * a * b, share * gcos * a * a,
         jnp.sum(share * gcos, axis=0, keepdims=True), jnp.zeros((1, GA), F32), u[8:16]], axis=0)
    cps = []
    for m, e in groups:
        cp = remote(wall.at[me], wall.at[me], s3_s.at[m, e], s3_r.at[m, e], group(m, e))
        cp.start()
        cps.append(cp)
        pending.append(cp)
    for (m, e) in groups:
        other = flip(z, m) * 2 + flip(c, e)
        remote(wall.at[other], wall.at[other], s3_s.at[m, e], s3_r.at[m, e], group(m, e)).wait_recv()

    lead = -(wcol * inv_pred * inv_meas)
    back = wcol * spot_cos * inv_pred * inv_pred
    dot1 = jnp.zeros((S, 1), F32)
    gene_total = jnp.zeros((1, GA), F32)
    for j in range(A):
        lanes = slice(j * GA, (j + 1) * GA)
        w = wall[j]
        direct = mcol[0] * w[0:1] + mcol[1] * w[1:2] + mcol[2] * w[2:3]
        damp = mcol[0] * w[3:4] + mcol[1] * w[4:5] + mcol[2] * w[5:6]
        gene_total = gene_total + w[6:7]
        p = pred[:, lanes]
        g = (lead - direct) * meas[:, lanes].astype(F32) + (back + damp) * p
        glow = g.astype(BF16)
        gp[0, 0, :, lanes] = glow
        dot1 = dot1 + jnp.sum(glow.astype(F32) * p, axis=1, keepdims=True)

    gz, gc = {}, {}

    def to_core(m):
        cp = remote(gp.at[m, 0], gp.at[m, 1], gc_s.at[m], gc_r.at[m], group(0, 1))
        cp.start()
        gc[m] = cp
        pending.append(cp)

    def to_plane(m, b):
        t = m ^ (1 << b)
        cp = remote(gp.at[m, 0], gp.at[t, 0], gz_s.at[t], gz_r.at[t], group(1 << b, 0))
        cp.start()
        gz[t] = cp
        pending.append(cp)

    for b in reversed(range(k.LV)):
        to_plane(0, b)
    to_core(0)

    for m, e in groups:
        dcp[m, e].wait_recv()
    dtot = dpart[0, 0]
    for m, e in groups:
        dtot = dtot + din[m, e]
    dot_row = jnp.broadcast_to(dot1, (S, S)).T[0:8] - dtot
    info2[0, 0] = dot_row
    i2 = {}
    for m, e in groups:
        cp = remote(info2.at[0, 0], info2.at[m, e], i2_s.at[m, e], i2_r.at[m, e], group(m, e))
        cp.start()
        i2[m, e] = cp
        pending.append(cp)

    fin = wall[0]
    total_tally = jnp.sum(tally, axis=0, keepdims=True)
    gsum = jnp.sum(gene_total, axis=1, keepdims=True)
    dens = jnp.zeros((1, 1), F32)
    for s in range(SLIDES):
        dens = dens + tally[s:s + 1] * fin[9:10, 1 + s:2 + s]
    lid = lax.broadcasted_iota(jnp.int32, (8, 128), 1)
    out_loss[...] = (jnp.where(lid == 0, fin[9:10, 0:1], 0.0) + jnp.where(lid == 1, gsum, 0.0)
                     + jnp.where(lid == 2, dens, 0.0)) / total_tally

    ycp = {}

    def map_piece(m):
        for e in range(2):
            if (m, e) != (0, 0):
                i2[m, e].wait_recv()
        gpm = gp.at[m]

        def step(i, _):
            r0 = pl.multiple_of(i * RC, RC)
            low = lax.dot_general(cells[pl.ds(r0, RC), :], gpm[...].reshape(2 * S, G),
                                  (((1,), (1,)), ((), ())), preferred_element_type=F32)
            rt = lax.dot_general(ratio_hl[:, pl.ds(r0, RC)], mext[:, m * 2 * S:(m + 1) * 2 * S],
                                 (((0,), (0,)), ((), ())), preferred_element_type=F32)
            low = low - rt
            per = YR // RC
            for e in range(2):
                sh = shares_of(m, e, i) * float(k.CELLS)
                v = sh * (low[:, e * S:(e + 1) * S] - info2[m, e, 0:1, :])
                ybuf[(m * 2 + e) * X + i // per,
                     pl.ds(pl.multiple_of(lax.rem(i, per) * RC, RC), RC), :] = v.astype(BF16)
            return 0

        lax.fori_loop(0, NC // RC, step, 0)
        for e in range(2):
            src = ybuf.at[pl.ds((m * 2 + e) * X, X)]
            if (m, e) == (0, 0):
                cp = pltpu.make_async_copy(src, out_map.at[z, :, c], loc_sem.at[3])
                cp.start()
                ycp[m, e] = cp
            else:
                cp = remote(src, out_map.at[z, :, c], y_s.at[m, e], y_r.at[m, e], group(m, e))
                cp.start()
                ycp[m, e] = cp
                pending.append(cp)

    gc[0].wait_recv()
    map_piece(0)
    held = [0, high]
    for b in reversed(range(k.LV)):
        for m in range(1 << b, Z, 2 << b):
            gz[m].wait_recv()
            for b2 in reversed(range(b)):
                to_plane(m, b2)
            to_core(m)
    for m in [high] + far:
        gc[m].wait_recv()
        map_piece(m)

    for m in near:
        gc[m].wait_recv()

    def slot_of(dx, dy, half):
        return ((dx * Y + dy) - 1) * 2 + half

    def single_rows(dx, dy, half):
        bx = lax.rem(x + dx, X)
        by = flip(y, dy)
        return pl.multiple_of(((bx * Y + by) * 2 + half) * H, H)

    def single_part(dx, dy, half, put):
        r0 = single_rows(dx, dy, half)

        def step(i, _):
            lanes = pl.ds(pl.multiple_of(i * NN, NN), NN)
            v = jnp.dot(slow[pl.ds(r0, H), :], gp[:, :, :, lanes].reshape(A * S, NN),
                        preferred_element_type=F32)
            put(lanes, v)
            return 0

        lax.fori_loop(0, G // NN, step, 0)

    def put_send(slot, extra=()):
        def put(lanes, v):
            for i in extra:
                v = v + grecv[i, :, lanes].astype(F32)
            gsend[slot, :, lanes] = v.astype(BF16)
        return put

    r_m1 = lambda d: d
    r_m2 = lambda d: XN + d
    r_m3 = lambda d: 2 * XN + d
    r_m5 = lambda d: 3 * XN + d
    r_m4, r_m6 = 4 * XN, 4 * XN + 1
    gcp = {}

    def send_single(slot, r_slot, where):
        cp = remote(gsend.at[slot], grecv.at[r_slot], gs_s.at[r_slot], gs_r.at[r_slot], where)
        cp.start()
        gcp[r_slot] = cp
        pending.append(cp)

    for d in range(XN):
        s0, s1_ = slot_of(d + 1, 1, 0), slot_of(d + 1, 1, 1)
        single_part(d + 1, 1, 0, put_send(s0))
        send_single(s0, r_m1(d), plane(d + 1, 0))
        single_part(d + 1, 1, 1, put_send(s1_))
        send_single(s1_, r_m2(d), plane(0, 1))
    for d in range(XN):
        s0 = slot_of(d + 1, 0, 0)
        single_part(d + 1, 0, 0, put_send(s0))
        send_single(s0, r_m3(d), plane(d + 1, 0))
    s0 = slot_of(0, 1, 1)
    single_part(0, 1, 1, put_send(s0))
    send_single(s0, r_m4, plane(0, 1))

    for m in near:
        map_piece(m)

    for d in range(XN):
        gcp[r_m2(d)].wait_recv()
        s0 = slot_of(d + 1, 0, 1)
        single_part(d + 1, 0, 1, put_send(s0, [r_m2(d)]))
        send_single(s0, r_m5(d), plane(d + 1, 0))
    for d in range(XN):
        gcp[r_m1(d)].wait_recv()
    s0 = slot_of(0, 1, 0)
    single_part(0, 1, 0, put_send(s0, [r_m1(d) for d in range(XN)]))
    send_single(s0, r_m6, plane(0, 1))

    def put_own(half):
        def put(lanes, v):
            out_single[half * H:(half + 1) * H, lanes] = v
        return put

    for half in range(2):
        single_part(0, 0, half, put_own(half))
    halves = [[r_m3(d) for d in range(XN)] + [r_m6], [r_m5(d) for d in range(XN)] + [r_m4]]
    for half in range(2):
        for i in halves[half]:
            gcp[i].wait_recv()

        def step(i, _):
            lanes = pl.ds(pl.multiple_of(i * NN, NN), NN)
            v = out_single[half * H:(half + 1) * H, lanes]
            for i2_ in halves[half]:
                v = v + grecv[i2_, :, lanes].astype(F32)
            out_single[half * H:(half + 1) * H, lanes] = v
            return 0

        lax.fori_loop(0, G // NN, step, 0)

    for m, e in groups:
        other = (flip(z, m), slice(None), flip(c, e))
        remote(ybuf.at[pl.ds(0, X)], out_map.at[other[0], :, other[2]], y_s.at[m, e], y_r.at[m, e],
               group(m, e)).wait_recv()
    ycp[0, 0].wait()
    for cp in pending:
        cp.wait_send()


def forward_and_back(k, logits, single_cell, spatial, ids, mask, cell_prior, order):
    Z, X, Y, A, Q, S, G, R, H = k.Z, k.X, k.Y, k.A, k.Q, k.S, k.G, k.R, k.H
    YR, NC, GA, XN = k.YR, k.NC, k.GA, k.X - 1
    vm = pl.BlockSpec(memory_space=pltpu.VMEM)
    hbm = pl.BlockSpec(memory_space=pl.ANY)
    dma = lambda *s: pltpu.SemaphoreType.DMA(s)
    ncl, ngs = 4 * XN + 2, 4 * XN + 2
    scratch = [
        pltpu.VMEM((Z, 2, X, YR, S), BF16),
        pltpu.VMEM((NC, G), BF16),
        pltpu.VMEM((NC, A * S), BF16),
        pltpu.VMEM((2 * S, NC), BF16),
        pltpu.VMEM((A * X, YR, S), BF16),
        pltpu.VMEM((Z, 2, 8, S), F32),
        pltpu.VMEM((Z, 2, 8, S), F32),
        pltpu.VMEM((Z, S, G), F32),
        pltpu.VMEM((Z, S, G), BF16),
        pltpu.VMEM((Z, S, G), BF16),
        pltpu.VMEM((Z - 1, S, G), BF16),
        pltpu.VMEM((Z - 1, S, G), BF16),
        pltpu.VMEM((S, G), F32),
        pltpu.VMEM((S, G), BF16),
        pltpu.VMEM((Z, 2, S, G), BF16),
        pltpu.VMEM((2 * (Q - 1), H, G), BF16),
        pltpu.VMEM((ngs, H, G), BF16),
        pltpu.VMEM((8, NC), F32),
        pltpu.VMEM((Q - 1, 8, NC), F32),
        pltpu.VMEM((16, NC), BF16),
        pltpu.VMEM((16, A * S), BF16),
        pltpu.VMEM((Z, 2, 8, S), F32),
        pltpu.VMEM((Z, 2, 8, S), F32),
        pltpu.VMEM((A, 16, GA), F32),
        pltpu.VMEM((Z, 2, 16, GA), F32),
        pltpu.VMEM((16, GA), F32),
        pltpu.VMEM((Q - 1, 16, GA), F32),
        pltpu.VMEM((A, 16, GA), F32),
        dma(4),
        dma(Z, 2), dma(Z, 2),
        dma(ncl), dma(ncl),
        dma(Z, 2), dma(Z, 2),
        dma(Z), dma(Z),
        dma(Z - 1), dma(Z - 1),
        dma(Q - 1), dma(Q - 1),
        dma(Z, 2), dma(Z, 2),
        dma(Z, 2), dma(Z, 2),
        dma(Q - 1), dma(Q - 1),
        dma(Z, 2), dma(Z, 2),
        dma(Z), dma(Z),
        dma(Z), dma(Z),
        dma(Z, 2), dma(Z, 2),
        dma(Z, 2), dma(Z, 2),
        dma(ngs), dma(ngs),
    ]
    return pl.pallas_call(
        functools.partial(kernel, k),
        name="mapping",
        out_shape=[
            jax.ShapeDtypeStruct((Z, X, 2, YR, S), BF16),
            jax.ShapeDtypeStruct((R, G), F32),
            jax.ShapeDtypeStruct((8, 128), F32),
        ],
        in_specs=[hbm, hbm, hbm, vm, vm, vm, vm, vm],
        out_specs=[hbm, vm, vm],
        scratch_shapes=scratch,
        compiler_params=pltpu.CompilerParams(
            collective_id=0, has_side_effects=True, vmem_limit_bytes=64000 * 1024),
        cost_estimate=pl.CostEstimate(
            flops=6 * NC * A * S * G, bytes_accessed=32 << 20, transcendentals=2 * NC * A * S),
    )(logits.reshape(Z, X, 2, YR, S), logits.reshape(A * X, YR, S), single_cell, spatial,
      ids.reshape(1, S), mask.reshape(1, S), cell_prior.reshape(A * X, YR), order.reshape(1, k.NB))


def body(mesh, map_logits, single_cell, spatial, slide_ids, spot_mask, cell_prior, gene_order):
    cells, spots = map_logits.shape
    k = Sizes(mesh, cells, spatial.shape[1], spots, gene_order.shape[0])
    gmap, gsingle, loss = forward_and_back(
        k, map_logits, single_cell, spatial, slide_ids, spot_mask, cell_prior, gene_order)
    grad_map = gmap.reshape(cells, spots).astype(F32)
    return loss[0, :3], grad_map, gsingle * float(cells) ** 0.5


def solution(mesh):
    k = Sizes(mesh, 1 << 20, 1 << 20, 128, 1)
    fine = Mesh(mesh.devices.reshape(k.Z, k.X, 2, k.Y), AXES)
    in_specs = (P(None, AXES), P(AXES, None), P(AXES, None), P(AXES), P(AXES), P(), P())
    out_specs = (P(), P(None, AXES), P(AXES, None))
    return jax.shard_map(functools.partial(body, mesh), mesh=fine, in_specs=in_specs,
                         out_specs=out_specs, check_vma=False)
```

time: 3470 us -> 315 us (0.09)
  waiting for transfers between devices: 3210 us -> 0 us
  Pallas kernels: 0 us -> 303 us
  matrix products: 168 us -> 0 us
  blocking collectives: 40.3 us -> 0 us
    unnamed x7 -> x0, waiting for transfers between devices: 2720 us -> none
    all_gather x4 -> x0, waiting for transfers between devices: 410 us -> none  [body(): lax.all_gather(local_block, ('spot', 'grp'), axis=0, tiled=True)]
    pallas_call x0 -> x1, Pallas kernels: none -> 303 us  [forward_and_back(): pl.pallas_call(functools.partial(kernel, k), name='mapping', out_shape=[j...]
    dot_general x25 -> x0, matrix products: 168 us -> none  [the longest x4 50.8 us: cell_terms(): lax.dot_general(portion, grad_block, (((1,), (1,)), ((), ())), preferred_...]
    psum x1 -> x0, waiting for transfers between devices: 75.2 us -> none  [body(): lax.psum((local_mass, local_tally, local_spot), ('spot', 'grp'))]
    psum x1 -> x0, blocking collectives: 40.3 us -> none  [body(): lax.psum((block_stats[0], block_stats[1], block_stats[2]), ('spot', 'grp'))]
  transfers between devices with their start and end apart: 6 -> 0, of which waited for: 6 -> 0; matrix products, arithmetic and copies ran while one was open for 4% -> 0% of each run, Pallas kernels for 0% -> 0%
where the time goes in v1:
time: 315 us
  Pallas kernels  303 us (96%)
  other arithmetic  8.89 us (3%)
    pallas_call x1, Pallas kernels, forward_and_back(): pl.pallas_call(functools.partial(kernel, k), name='mapping', out_shape=[j...  303 us

profile of v1, /device:TPU:9, one launch (start us, length us, event | category | flops | bytes accessed | tf_op | source)
XLA Modules:
  0.0 315.1 jit_solution(1459385815692287777)
XLA Ops:
  0.6 1.5 reshape.31.cell_prior
  2.1 302.9 %mapping.1 = (bf16[4,2,2,1024,128]{4,3,2,1,0:T(8,128)(2,1)}, f32[512,2048]{1,0:T(8,128)}, f32[8,128]{1,0:T(8,128)}) custom-call(bf16[4,2,2,1024,128]{4,3,2,1,0:T(8,128)(2,1)} %bitcast.10, bf16[16,1024,128]{2,1,0:T(8,128)(2,1)} %bitcast.11, bf16[512,2048]{1,0:T(8,128)(2,1)} %own_cells.1, bf16[128,2048]{1,0:T(8,128)(2,1)} %spatial.1, s32[1,128]{1,0:T(1,128)} %bitcast.12, ...), custom_call_target="tpu_custom_call" | custom-call | flops 25769803776 | bytes 33554432 | tf_op jit(solution)/shard_map/mapping/pallas_call | solution.py:631
  305.0 1.2 slice_bitcast_fusion
  306.2 0.0 copy-start
  306.2 4.9 %broadcast_multiply_fusion = f32[512,2048]{1,0:T(8,128)} fusion(f32[512,2048]{1,0:T(8,128)} %get-tuple-element.8), kind=kLoop, calls=%fused_computation.1 | loop fusion | flops 1048576 | bytes 8388608 | tf_op jit(solution)/shard_map/mul | solution.py:656
  311.2 0.0 copy-done
  311.2 4.0 %bitcast_convert_fusion = f32[16384,128]{1,0:T(8,128)} fusion(bf16[4,2,2,1024,128]{4,3,2,1,0:T(8,128)(2,1)S(1)} %copy-done), kind=kLoop, calls=%fused_computation | loop fusion | flops 2097152 | bytes 12582912 | tf_op jit(solution)/shard_map/convert_element_type | solution.py:655
Async XLA Ops:
  306.2 4.9 %copy-start = (bf16[4,2,2,1024,128]{4,3,2,1,0:T(8,128)(2,1)S(1)}, bf16[4,2,2,1024,128]{4,3,2,1,0:T(8,128)(2,1)}, u32[]{:S(2)}) copy-start(bf16[4,2,2,1024,128]{4,3,2,1,0:T(8,128)(2,1)} %get-tuple-element.7) | copy-start | bytes 12582916

commit v2 on v1

--- a/solution.py
+++ b/solution.py
@@ -42,13 +42,14 @@
         self.NC = self.X * self.YR
         self.GA = genes // self.A
         self.RC = min(256, self.YR)
+        self.PL = min(128, self.YR)
         self.NN = min(512, genes)
 
 
 def kernel(k, logits, logits_flat, own_cells, spatial, ids, mask, cell_prior, order,
            out_map, out_single, out_loss,
            lbuf, cells, slow, slow_t, ybuf, info, info2,
-           pacc, p1, psib, rs_out, rs_in, pred, meas,
+           pacc, p1, psib, rs_out, rs_in, meas,
            gp, gsend, grecv,
            mass_out, mass_in, ratio_hl, mext, dpart, din,
            stat, s1, ubuf, s2, wall,
@@ -61,7 +62,7 @@
     yo = 1 - y
 
     def group(m, e):
-        return (flip(z, m), x, flip(c, e), y)
+        return (flip(z, m), x, c + e - 2 * c * e, y)
 
     def plane(dx, dy):
         return (z, lax.rem(x + dx, X), c, flip(y, dy))
@@ -118,10 +119,10 @@
     high = Z // 2
     far = [m for m in range(Z) if m & high and m != high]
     near = [m for m in range(1, Z) if not m & high]
+    send_logits(0, 1)
     for m in far + near + [high]:
         for e in range(2):
             send_logits(m, e)
-    send_logits(0, 1)
     for cp in x_last + [y_last]:
         cp.start()
     pending.extend(x_first + x_last + [y_first, y_last])
@@ -185,6 +186,10 @@
         l = lbuf[m, e, i // per, pl.ds(pl.multiple_of(lax.rem(i, per) * RC, RC), RC), :]
         return jnp.exp(l.astype(F32)) * info[m, e, 0:1, :]
 
+    def t_row(m, e):
+        m = 0 if m == high else m - (m > high)
+        return (m * 2 + e) * S
+
     def make_shares(m):
         for e in range(2):
             if (m, e) != (0, 0):
@@ -197,7 +202,7 @@
                 sh = shares_of(m, e, i)
                 r0 = pl.multiple_of(i * RC, RC)
                 slow[pl.ds(r0, RC), lane:lane + S] = sh.astype(BF16)
-                slow_t[e * S:(e + 1) * S, pl.ds(r0, RC)] = sh.T.astype(BF16)
+                slow_t[t_row(m, e):t_row(m, e) + S, pl.ds(r0, RC)] = sh.astype(BF16).T
                 return 0
 
             lax.fori_loop(0, NC // RC, step, 0)
@@ -205,7 +210,8 @@
     def predict(m):
         def step(i, _):
             lanes = pl.ds(pl.multiple_of(i * NN, NN), NN)
-            r = jnp.dot(slow_t[...], cells[:, lanes], preferred_element_type=F32)
+            r = jnp.dot(slow_t[t_row(m, 0):t_row(m, 0) + 2 * S, :], cells[:, lanes],
+                        preferred_element_type=F32)
             pacc[m, :, lanes] = r[:S]
             p1[m, :, lanes] = r[S:].astype(BF16)
             return 0
@@ -215,16 +221,6 @@
         cp.start()
         pending.append(cp)
         return cp
-
-    ps = {}
-    first = True
-    for m in far + near + [0, high] if Z > 2 else [0, high]:
-        make_shares(m)
-        if first:
-            for cp in x_last + [y_last] + fwd_a + fwd_b:
-                cp.wait_recv()
-            first = False
-        ps[m] = predict(m)
 
     rs = {}
 
@@ -244,18 +240,32 @@
             return t
         return total
 
-    for b in range(k.LV):
+    def send_level(b):
         step_m = 1 << b
-        ms = [m for m in range(step_m, Z, 2 * step_m)]
-        for m in reversed(ms):
+        for m in reversed(range(step_m, Z, 2 * step_m)):
             total = piece_sum(m, b)
             slot = level_slot(b, m ^ step_m)
-            rs_out[slot] = total(slice(0, G)).astype(BF16)
+            for j in range(A):
+                lanes = slice(j * GA, (j + 1) * GA)
+                rs_out[slot, :, lanes] = total(lanes).astype(BF16)
             cp = remote(rs_out.at[slot], rs_in.at[slot], rs_s.at[slot], rs_r.at[slot],
                         group(step_m, 0))
             cp.start()
             rs[b, m ^ step_m] = cp
             pending.append(cp)
+
+    ps = {}
+    for m in [0] + far + near:
+        make_shares(m)
+    for cp in x_last + [y_last] + fwd_a + fwd_b:
+        cp.wait_recv()
+    for b in range(k.LV):
+        if b == k.LV - 1:
+            ps[0] = predict(0)
+            make_shares(high)
+        for m in reversed(range(1 << b, Z, 2 << b)):
+            ps[m] = predict(m)
+        send_level(b)
 
     mem_rows = jnp.concatenate(
         [info[m, e, 1:1 + SLIDES, :] for m in range(Z) for e in range(2)], axis=1)
@@ -280,7 +290,8 @@
     quota = mass / tally
     prior_sum = jnp.sum(jnp.sum(cell_prior[...], axis=0, keepdims=True), axis=1, keepdims=True)
     prior = jnp.concatenate(
-        [cell_prior[pl.ds((z * X + bx) * 2 + c, 1), :] for bx in range(X)], axis=1) / prior_sum
+        [cell_prior[pl.ds(((z * X + bx) * 2 + c) * (YR // k.PL) + i, 1), :]
+         for bx in range(X) for i in range(YR // k.PL)], axis=1) / prior_sum
     kl = jnp.sum(prior * (jnp.log(prior) - jnp.log(quota)), axis=1, keepdims=True)
     rat = prior / quota
     rat_hi = rat.astype(BF16)
@@ -310,7 +321,7 @@
     for j in range(A):
         lanes = slice(j * GA, (j + 1) * GA)
         p = total(lanes)
-        pred[:, lanes] = p
+        pacc[0, :, lanes] = p
         q = meas[:, lanes].astype(F32)
         pq, pp = p * q, p * p
         pred_sq = pred_sq + jnp.sum(pp, axis=1, keepdims=True)
@@ -375,7 +386,7 @@
         direct = mcol[0] * w[0:1] + mcol[1] * w[1:2] + mcol[2] * w[2:3]
         damp = mcol[0] * w[3:4] + mcol[1] * w[4:5] + mcol[2] * w[5:6]
         gene_total = gene_total + w[6:7]
-        p = pred[:, lanes]
+        p = pacc[0, :, lanes]
         g = (lead - direct) * meas[:, lanes].astype(F32) + (back + damp) * p
         glow = g.astype(BF16)
         gp[0, 0, :, lanes] = glow
@@ -396,9 +407,17 @@
         gz[t] = cp
         pending.append(cp)
 
-    for b in reversed(range(k.LV)):
+    top = k.LV - 1
+    to_core(0)
+    gz[high] = remote(gp.at[0, 0], gp.at[high, 0], gz_s.at[high], gz_r.at[high], group(high, 0))
+    pending.append(gz[high])
+
+    @pl.when(c == 0)
+    def _():
+        gz[high].start()
+
+    for b in reversed(range(top)):
         to_plane(0, b)
-    to_core(0)
 
     for m, e in groups:
         dcp[m, e].wait_recv()
@@ -426,54 +445,91 @@
 
     ycp = {}
 
+    def map_rows(m, es, gpm):
+        n = len(es)
+
+        def step(i, _):
+            r0 = pl.multiple_of(i * RC, RC)
+            low = lax.dot_general(cells[pl.ds(r0, RC), :], gpm(),
+                                  (((1,), (1,)), ((), ())), preferred_element_type=F32)
+            mx = [mext[:, pl.ds(pl.multiple_of((m * 2 + e) * S, S), S)] for e in es]
+            rt = lax.dot_general(ratio_hl[:, pl.ds(r0, RC)], jnp.concatenate(mx, axis=1),
+                                 (((0,), (0,)), ((), ())), preferred_element_type=F32)
+            low = low - rt
+            per = YR // RC
+            for i_e, e in enumerate(es):
+                sh = shares_of(m, e, i) * float(k.CELLS)
+                v = sh * (low[:, i_e * S:(i_e + 1) * S] - info2[m, e, 0:1, :])
+                ybuf[(m * 2 + e) * X + i // per,
+                     pl.ds(pl.multiple_of(lax.rem(i, per) * RC, RC), RC), :] = v.astype(BF16)
+            return 0
+
+        lax.fori_loop(0, NC // RC, step, 0)
+        for e in es:
+            src = ybuf.at[pl.ds((m * 2 + e) * X, X)]
+            if m == 0 and type(e) is int and e == 0:
+                cp = pltpu.make_async_copy(src, out_map.at[z, :, c], loc_sem.at[3])
+                cp.start()
+                ycp[0, 0] = cp
+            else:
+                cp = remote(src, out_map.at[z, :, c], y_s.at[m, e], y_r.at[m, e], group(m, e))
+                cp.start()
+                pending.append(cp)
+
     def map_piece(m):
         for e in range(2):
             if (m, e) != (0, 0):
                 i2[m, e].wait_recv()
-        gpm = gp.at[m]
-
-        def step(i, _):
-            r0 = pl.multiple_of(i * RC, RC)
-            low = lax.dot_general(cells[pl.ds(r0, RC), :], gpm[...].reshape(2 * S, G),
-                                  (((1,), (1,)), ((), ())), preferred_element_type=F32)
-            rt = lax.dot_general(ratio_hl[:, pl.ds(r0, RC)], mext[:, m * 2 * S:(m + 1) * 2 * S],
-                                 (((0,), (0,)), ((), ())), preferred_element_type=F32)
-            low = low - rt
-            per = YR // RC
-            for e in range(2):
-                sh = shares_of(m, e, i) * float(k.CELLS)
-                v = sh * (low[:, e * S:(e + 1) * S] - info2[m, e, 0:1, :])
-                ybuf[(m * 2 + e) * X + i // per,
-                     pl.ds(pl.multiple_of(lax.rem(i, per) * RC, RC), RC), :] = v.astype(BF16)
-            return 0
-
-        lax.fori_loop(0, NC // RC, step, 0)
-        for e in range(2):
-            src = ybuf.at[pl.ds((m * 2 + e) * X, X)]
-            if (m, e) == (0, 0):
-                cp = pltpu.make_async_copy(src, out_map.at[z, :, c], loc_sem.at[3])
-                cp.start()
-                ycp[m, e] = cp
-            else:
-                cp = remote(src, out_map.at[z, :, c], y_s.at[m, e], y_r.at[m, e], group(m, e))
-                cp.start()
-                ycp[m, e] = cp
-                pending.append(cp)
+        map_rows(m, [0, 1], lambda: gp[m].reshape(2 * S, G))
 
     gc[0].wait_recv()
     map_piece(0)
-    held = [0, high]
-    for b in reversed(range(k.LV)):
+
+    def pass_on(m, b):
+        for b2 in reversed(range(b)):
+            to_plane(m, b2)
+        to_core(m)
+
+    gc[high] = remote(gp.at[high, 0], gp.at[high, 1], gc_s.at[high], gc_r.at[high], group(0, 1))
+    pending.append(gc[high])
+    for b2 in range(top):
+        t = high ^ (1 << b2)
+        gz[t] = remote(gp.at[high, 0], gp.at[t, 0], gz_s.at[t], gz_r.at[t], group(1 << b2, 0))
+        pending.append(gz[t])
+
+    def high_on():
+        gz[high].wait_recv()
+        gc[high].start()
+        for b2 in reversed(range(top)):
+            gz[high ^ (1 << b2)].start()
+
+    @pl.when(c == 0)
+    def _():
+        high_on()
+
+    @pl.when(c == 1)
+    def _():
+        gc[high].wait_recv()
+        gz[high].start()
+
+    i2[high, 0].wait_recv()
+    i2[high, 1].wait_recv()
+    map_rows(high, [c], lambda: gp[high, c])
+
+    @pl.when(c == 1)
+    def _():
+        high_on()
+
+    @pl.when(c == 0)
+    def _():
+        gc[high].wait_recv()
+
+    map_rows(high, [1 - c], lambda: gp[high, 1 - c])
+    for b in reversed(range(top)):
         for m in range(1 << b, Z, 2 << b):
             gz[m].wait_recv()
-            for b2 in reversed(range(b)):
-                to_plane(m, b2)
-            to_core(m)
-    for m in [high] + far:
-        gc[m].wait_recv()
-        map_piece(m)
-
-    for m in near:
+            pass_on(m, b)
+    for m in far + near:
         gc[m].wait_recv()
 
     def slot_of(dx, dy, half):
@@ -522,6 +578,8 @@
         send_single(s0, r_m1(d), plane(d + 1, 0))
         single_part(d + 1, 1, 1, put_send(s1_))
         send_single(s1_, r_m2(d), plane(0, 1))
+    for m in far:
+        map_piece(m)
     for d in range(XN):
         s0 = slot_of(d + 1, 0, 0)
         single_part(d + 1, 0, 0, put_send(s0))
@@ -561,7 +619,7 @@
             v = out_single[half * H:(half + 1) * H, lanes]
             for i2_ in halves[half]:
                 v = v + grecv[i2_, :, lanes].astype(F32)
-            out_single[half * H:(half + 1) * H, lanes] = v
+            out_single[half * H:(half + 1) * H, lanes] = v * float(k.CELLS) ** 0.5
             return 0
 
         lax.fori_loop(0, G // NN, step, 0)
@@ -586,7 +644,7 @@
         pltpu.VMEM((Z, 2, X, YR, S), BF16),
         pltpu.VMEM((NC, G), BF16),
         pltpu.VMEM((NC, A * S), BF16),
-        pltpu.VMEM((2 * S, NC), BF16),
+        pltpu.VMEM(((A - 2) * S, NC), BF16),
         pltpu.VMEM((A * X, YR, S), BF16),
         pltpu.VMEM((Z, 2, 8, S), F32),
         pltpu.VMEM((Z, 2, 8, S), F32),
@@ -595,7 +653,6 @@
         pltpu.VMEM((Z, S, G), BF16),
         pltpu.VMEM((Z - 1, S, G), BF16),
         pltpu.VMEM((Z - 1, S, G), BF16),
-        pltpu.VMEM((S, G), F32),
         pltpu.VMEM((S, G), BF16),
         pltpu.VMEM((Z, 2, S, G), BF16),
         pltpu.VMEM((2 * (Q - 1), H, G), BF16),
@@ -644,7 +701,7 @@
         cost_estimate=pl.CostEstimate(
             flops=6 * NC * A * S * G, bytes_accessed=32 << 20, transcendentals=2 * NC * A * S),
     )(logits.reshape(Z, X, 2, YR, S), logits.reshape(A * X, YR, S), single_cell, spatial,
-      ids.reshape(1, S), mask.reshape(1, S), cell_prior.reshape(A * X, YR), order.reshape(1, k.NB))
+      ids.reshape(1, S), mask.reshape(1, S), cell_prior.reshape(-1, k.PL), order.reshape(1, k.NB))
 
 
 def body(mesh, map_logits, single_cell, spatial, slide_ids, spot_mask, cell_prior, gene_order):
@@ -653,7 +710,7 @@
     gmap, gsingle, loss = forward_and_back(
         k, map_logits, single_cell, spatial, slide_ids, spot_mask, cell_prior, gene_order)
     grad_map = gmap.reshape(cells, spots).astype(F32)
-    return loss[0, :3], grad_map, gsingle * float(cells) ** 0.5
+    return loss[0, :3], grad_map, gsingle
 
 
 def solution(mesh):

time: 315 us -> 293 us (0.930)
  Pallas kernels: 303 us -> 282 us
  other arithmetic: 8.89 us -> 5.41 us
    pallas_call x1, Pallas kernels: 303 us -> 282 us  [forward_and_back(): pl.pallas_call(functools.partial(kernel, k), name='mapping', out_shape=[j...]
    mul x1 -> x0, other arithmetic: 4.94 us -> none  [body(): return (loss[0, :3], grad_map, gsingle * float(cells) ** 0.5)]
where the time goes in v2:
time: 293 us; the launch traced here: 291 us
  Pallas kernels  282 us (96%)
  other arithmetic  5.41 us (2%)
  local copies, waits for them, and re-layouts  3.21 us (1%)
    pallas_call x1, Pallas kernels, forward_and_back(): pl.pallas_call(functools.partial(kernel, k), name='mapping', out_shape=[j...  282 us

profile of v2, /device:TPU:9, one launch (start us, length us, event | category | flops | bytes accessed | tf_op | source)
XLA Modules:
  0.0 291.0 jit_solution(12022617531998294093)
XLA Ops:
  0.6 281.7 %mapping.1 = (bf16[4,2,2,1024,128]{4,3,2,1,0:T(8,128)(2,1)}, f32[512,2048]{1,0:T(8,128)}, f32[8,128]{1,0:T(8,128)}) custom-call(bf16[4,2,2,1024,128]{4,3,2,1,0:T(8,128)(2,1)} %bitcast.11, bf16[16,1024,128]{2,1,0:T(8,128)(2,1)} %bitcast.12, bf16[512,2048]{1,0:T(8,128)(2,1)} %own_cells.1, bf16[128,2048]{1,0:T(8,128)(2,1)} %spatial.1, s32[1,128]{1,0:T(1,128)} %bitcast.14, ...), custom_call_target="tpu_custom_call" | custom-call | flops 25769803776 | bytes 33554432 | tf_op jit(solution)/shard_map/mapping/pallas_call | solution.py:688
  282.4 1.2 slice_bitcast_fusion
  283.5 0.0 copy-start
  283.5 5.4 %bitcast_convert_fusion = f32[16384,128]{1,0:T(8,128)} fusion(bf16[4,2,2,1024,128]{4,3,2,1,0:T(8,128)(2,1)} %get-tuple-element.7), kind=kLoop, calls=%fused_computation | loop fusion | flops 2097152 | bytes 12582912 | tf_op jit(solution)/shard_map/convert_element_type | solution.py:712
  289.0 0.0 copy-done
  289.0 2.0 copy.11
Async XLA Ops:
  283.5 5.4 %copy-start = (f32[512,2048]{1,0:T(8,128)S(1)}, f32[512,2048]{1,0:T(8,128)}, u32[]{:S(2)}) copy-start(f32[512,2048]{1,0:T(8,128)} %get-tuple-element.14) | copy-start | bytes 12582916

commit v3 on v2

--- a/solution.py
+++ b/solution.py
@@ -49,13 +49,13 @@
 def kernel(k, logits, logits_flat, own_cells, spatial, ids, mask, cell_prior, order,
            out_map, out_single, out_loss,
            lbuf, cells, slow, slow_t, ybuf, info, info2,
-           pacc, p1, psib, rs_out, rs_in, meas,
+           pacc, p1, psib, rs_in, meas,
            gp, gsend, grecv,
            mass_out, mass_in, ratio_hl, mext, dpart, din,
-           stat, s1, ubuf, s2, wall,
+           mstat, mstat_in, stat, s1, ubuf, s2, wall, own_single,
            loc_sem, lg_s, lg_r, cl_s, cl_r, in_s, in_r, ps_s, ps_r, rs_s, rs_r, ms_s, ms_r,
            d_s, d_r, s1_s, s1_r, s2_s, s2_r, s3_s, s3_r, gz_s, gz_r, gc_s, gc_r, i2_s, i2_r,
-           y_s, y_r, gs_s, gs_r):
+           y_s, y_r, gs_s, gs_r, mt_s, mt_r, gate):
     Z, X, Y, A, Q, S, G, R, H = k.Z, k.X, k.Y, k.A, k.Q, k.S, k.G, k.R, k.H
     YR, NC, GA, RC, NN = k.YR, k.NC, k.GA, k.RC, k.NN
     z, x, c, y = [lax.axis_index(a) for a in AXES]
@@ -107,22 +107,36 @@
     for cp in x_first + [y_first]:
         cp.start()
 
-    lg = {}
-
-    def send_logits(m, e):
-        cp = remote(logits.at[flip(z, m), :, flip(c, e)], lbuf.at[m, e],
-                    lg_s.at[m, e], lg_r.at[m, e], group(m, e))
-        cp.start()
-        lg[m, e] = cp
-        pending.append(cp)
-
     high = Z // 2
     far = [m for m in range(Z) if m & high and m != high]
     near = [m for m in range(1, Z) if not m & high]
-    send_logits(0, 1)
-    for m in far + near + [high]:
-        for e in range(2):
-            send_logits(m, e)
+    lg = {(m, e): remote(logits.at[flip(z, m), :, flip(c, e)], lbuf.at[m, e],
+                         lg_s.at[m, e], lg_r.at[m, e], group(m, e)) for m, e in groups}
+
+    pending.extend(cp for (m, e), cp in lg.items() if m in [0] + near)
+
+    def sent(ms):
+        for m in ms:
+            for e in range(2):
+                lg[m, e].wait_send()
+
+    def send_logits(ms, es=(0, 1)):
+        for m in ms:
+            for e in es:
+                lg[m, e].start()
+
+    at_end = (z == 0) | (z == Z - 1)
+    inside = jnp.logical_not(at_end)
+    lg[0, 1].start()
+
+    @pl.when(at_end)
+    def _():
+        send_logits(near + far)
+
+    @pl.when(inside)
+    def _():
+        send_logits([high])
+
     for cp in x_last + [y_last]:
         cp.start()
     pending.extend(x_first + x_last + [y_first, y_last])
@@ -161,8 +175,15 @@
         v = v * v
         meas_sq = meas_sq + jnp.sum(v, axis=1, keepdims=True)
         for s in range(SLIDES):
-            stat[j, 6 + s:7 + s, :] = jnp.sum(mcol[s] * v, axis=0, keepdims=True)
+            mstat[j, s:s + 1, :] = jnp.sum(mcol[s] * v, axis=0, keepdims=True)
+        mstat[j, SLIDES:8, :] = jnp.zeros((8 - SLIDES, GA), F32)
     inv_meas = lax.rsqrt(meas_sq + FLOOR)
+    mst = {}
+    for m, e in groups:
+        mst[m, e] = remote(mstat.at[flip(z, m) * 2 + flip(c, e)], mstat_in.at[m, e],
+                           mt_s.at[m, e], mt_r.at[m, e], group(m, e))
+        mst[m, e].start()
+    pending.extend(mst.values())
 
     fwd_a, fwd_b = [], []
     for d in range(XN):
@@ -186,52 +207,105 @@
         l = lbuf[m, e, i // per, pl.ds(pl.multiple_of(lax.rem(i, per) * RC, RC), RC), :]
         return jnp.exp(l.astype(F32)) * info[m, e, 0:1, :]
 
-    def t_row(m, e):
-        m = 0 if m == high else m - (m > high)
-        return (m * 2 + e) * S
-
-    def make_shares(m):
+    def t_row(m, i):
+        return (m * 2 + i) * S
+
+    def slot(cc):
+        return c if cc == 0 else 1 - c
+
+    def wait_cross(m, cc):
+        e = slot(cc)
+        remote(info.at[0, 0], info.at[m, e], in_s.at[m, e], in_r.at[m, e],
+               group(m, e)).wait_recv()
+        remote(lbuf.at[0, 0], lbuf.at[m, e], lg_s.at[m, e], lg_r.at[m, e],
+               group(m, e)).wait_recv()
+
+    def wait_pair(m):
         for e in range(2):
             if (m, e) != (0, 0):
                 inf[m, e].wait_recv()
                 lg[m, e].wait_recv()
+
+    def make_shares(m, e, row):
+        lane = (m * 2 + e) * S
+        if type(e) is not int:
+            lane = pl.multiple_of(lane, S)
+
+        def step(i, _):
+            sh = shares_of(m, e, i).astype(BF16)
+            r0 = pl.multiple_of(i * RC, RC)
+            slow[pl.ds(r0, RC), pl.ds(lane, S)] = sh
+            slow_t[row:row + S, pl.ds(r0, RC)] = sh.T
+            return 0
+
+        lax.fori_loop(0, NC // RC, step, 0)
+
+    def pair_shares(m):
+        wait_pair(m)
         for e in range(2):
-            lane = (m * 2 + e) * S
-
-            def step(i, _):
-                sh = shares_of(m, e, i)
-                r0 = pl.multiple_of(i * RC, RC)
-                slow[pl.ds(r0, RC), lane:lane + S] = sh.astype(BF16)
-                slow_t[t_row(m, e):t_row(m, e) + S, pl.ds(r0, RC)] = sh.astype(BF16).T
-                return 0
-
-            lax.fori_loop(0, NC // RC, step, 0)
-
-    def predict(m):
+            make_shares(m, e, t_row(m, e))
+
+    def cross_shares(m, cc):
+        make_shares(m, slot(cc), t_row(m, cc))
+
+    ps = [remote(p1.at[m], psib.at[m], ps_s.at[m], ps_r.at[m], group(0, 1)) for m in range(Z)]
+    pending.extend(ps)
+
+    def gene_loop(put):
         def step(i, _):
-            lanes = pl.ds(pl.multiple_of(i * NN, NN), NN)
-            r = jnp.dot(slow_t[t_row(m, 0):t_row(m, 0) + 2 * S, :], cells[:, lanes],
-                        preferred_element_type=F32)
+            put(pl.ds(pl.multiple_of(i * NN, NN), NN))
+            return 0
+
+        lax.fori_loop(0, G // NN, step, 0)
+
+    def predict_pair(m):
+        row = t_row(m, 0)
+
+        def put(lanes):
+            r = jnp.dot(slow_t[row:row + 2 * S, :], cells[:, lanes], preferred_element_type=F32)
             pacc[m, :, lanes] = r[:S]
             p1[m, :, lanes] = r[S:].astype(BF16)
-            return 0
-
-        lax.fori_loop(0, G // NN, step, 0)
-        cp = remote(p1.at[m], psib.at[m], ps_s.at[m], ps_r.at[m], group(0, 1))
-        cp.start()
-        pending.append(cp)
-        return cp
-
-    rs = {}
+
+        gene_loop(put)
+        ps[m].start()
+
+    def predict_cross(m, cc):
+        row = t_row(m, cc)
+
+        def part(lanes):
+            return jnp.dot(slow_t[row:row + S, :], cells[:, lanes], preferred_element_type=F32)
+
+        @pl.when(c == cc)
+        def _():
+            def put(lanes):
+                pacc[m, :, lanes] = part(lanes)
+
+            gene_loop(put)
+
+        @pl.when(c != cc)
+        def _():
+            def put(lanes):
+                p1[m, :, lanes] = part(lanes).astype(BF16)
+
+            gene_loop(put)
+            ps[m].start()
 
     def level_slot(b, m):
         return sum(Z >> (j + 1) for j in range(b)) + (m >> (b + 1))
 
+    rs = {}
+    for b in range(k.LV):
+        step_m = 1 << b
+        for m in range(0, Z, 2 * step_m):
+            sl = level_slot(b, m)
+            rs[b, m] = remote(psib.at[m ^ step_m], rs_in.at[sl], rs_s.at[sl], rs_r.at[sl],
+                              group(step_m, 0))
+    pending.extend(rs.values())
+
     def piece_sum(m, b):
-        cps = [rs[j, m] for j in range(b)]
         ps[m].wait_recv()
-        for cp in cps:
-            cp.wait_recv()
+        for j in range(b):
+            rs[j, m].wait_recv()
 
         def total(lanes):
             t = pacc[m, :, lanes] + psib[m, :, lanes].astype(F32)
@@ -240,40 +314,119 @@
             return t
         return total
 
-    def send_level(b):
-        step_m = 1 << b
-        for m in reversed(range(step_m, Z, 2 * step_m)):
-            total = piece_sum(m, b)
-            slot = level_slot(b, m ^ step_m)
-            for j in range(A):
-                lanes = slice(j * GA, (j + 1) * GA)
-                rs_out[slot, :, lanes] = total(lanes).astype(BF16)
-            cp = remote(rs_out.at[slot], rs_in.at[slot], rs_s.at[slot], rs_r.at[slot],
-                        group(step_m, 0))
-            cp.start()
-            rs[b, m ^ step_m] = cp
-            pending.append(cp)
-
-    ps = {}
-    for m in [0] + far + near:
-        make_shares(m)
+    def sum_level(b, m):
+        total = piece_sum(m, b)
+        for j in range(A):
+            lanes = slice(j * GA, (j + 1) * GA)
+            psib[m, :, lanes] = total(lanes).astype(BF16)
+
+    def far_levels(cc):
+        @pl.when(c == cc)
+        def _():
+            for b in range(top):
+                send_level(b, of_level(b, far))
+
+    def send_level(b, ms):
+        for m in ms:
+            sum_level(b, m)
+            rs[b, m ^ (1 << b)].start()
+
+    top = k.LV - 1
+    def of_level(b, ms):
+        return [m for m in reversed(ms) if m % (2 << b) == 1 << b]
+
+    pair_shares(0)
+
+    @pl.when(at_end)
+    def _():
+        sent(far)
+        send_logits([high])
+
+    @pl.when(inside)
+    def _():
+        sent([high])
+        send_logits(near)
+
+    pair_shares(high)
+
+    @pl.when(inside & (c == 0))
+    def _():
+        send_logits(far)
+
+    @pl.when(at_end)
+    def _():
+        for m in far:
+            for cc in range(2):
+                wait_cross(m, cc)
+                cross_shares(m, cc)
+
+    for m in near:
+        pair_shares(m)
     for cp in x_last + [y_last] + fwd_a + fwd_b:
         cp.wait_recv()
-    for b in range(k.LV):
-        if b == k.LV - 1:
-            ps[0] = predict(0)
-            make_shares(high)
-        for m in reversed(range(1 << b, Z, 2 << b)):
-            ps[m] = predict(m)
-        send_level(b)
+
+    @pl.when(at_end)
+    def _():
+        for cc in range(2):
+            for m in far:
+                predict_cross(m, cc)
+        for cc in range(2):
+            far_levels(cc)
+
+    predict_pair(high)
+    for b in range(top):
+        for m in of_level(b, near):
+            predict_pair(m)
+        send_level(b, of_level(b, near))
+    predict_pair(0)
+
+    @pl.when(inside)
+    def _():
+        for m in far:
+            wait_cross(m, 0)
+
+        @pl.when(c == 1)
+        def _():
+            send_logits(far, (1, 0))
+
+        for m in far:
+            cross_shares(m, 0)
+            predict_cross(m, 0)
+        far_levels(0)
+
+        @pl.when(c == 0)
+        def _():
+            sum_level(top, high)
+
+        for m in far:
+            wait_cross(m, 1)
+            cross_shares(m, 1)
+            predict_cross(m, 1)
+
+        @pl.when(c == 0)
+        def _():
+            rs[top, 0].start()
+
+        far_levels(1)
+
+    @pl.when(at_end | (c == 1))
+    def _():
+        sum_level(top, high)
+        rs[top, 0].start()
 
     mem_rows = jnp.concatenate(
         [info[m, e, 1:1 + SLIDES, :] for m in range(Z) for e in range(2)], axis=1)
     mem16 = jnp.concatenate([mem_rows, jnp.zeros((16 - SLIDES, A * S), F32)], axis=0).astype(BF16)
     part = lax.dot_general(mem16, slow[...], (((1,), (1,)), ((), ())), preferred_element_type=F32)
     col_tally = jnp.sum(mem_rows, axis=1, keepdims=True)
+    gmeas = mstat[me]
+    for m, e in groups:
+        mst[m, e].wait_recv()
+        gmeas = gmeas + mstat_in[m, e]
+    packed = [gmeas[s:s + 1] for s in range(SLIDES)] + [jnp.zeros((1, NC - SLIDES * GA), F32)]
     mass_out[...] = jnp.concatenate(
-        [part[:SLIDES], jnp.broadcast_to(col_tally, (SLIDES, NC)), jnp.zeros((2, NC), F32)], axis=0)
+        [part[:SLIDES], jnp.broadcast_to(col_tally, (SLIDES, NC)),
+         jnp.concatenate(packed, axis=1), jnp.zeros((1, NC), F32)], axis=0)
     mcp = []
     for i, (dx, dy) in enumerate(planes):
         cp = remote(mass_out, mass_in.at[i], ms_s.at[i], ms_r.at[i], plane(dx, dy))
@@ -286,6 +439,9 @@
     for i in range(Q - 1):
         msum = msum + mass_in[i]
     mass = msum[:SLIDES]
+    gmeas = jnp.concatenate(
+        [msum[6:7, s * GA:(s + 1) * GA] for s in range(SLIDES)], axis=0)
+    inv_gmeas = lax.rsqrt(gmeas + FLOOR)
     tally = jnp.maximum(msum[SLIDES:2 * SLIDES, 0:1], 1.0)
     quota = mass / tally
     prior_sum = jnp.sum(jnp.sum(cell_prior[...], axis=0, keepdims=True), axis=1, keepdims=True)
@@ -336,7 +492,7 @@
     for s in range(SLIDES):
         scal = scal + jnp.where(lane_id == 1 + s, kl[s:s + 1] * (1.0 / Q), 0.0)
     for j in range(A):
-        stat[j, 9:16, :] = jnp.concatenate([scal, jnp.zeros((6, GA), F32)], axis=0)
+        stat[j, 6:8, :] = jnp.concatenate([scal, jnp.zeros((1, GA), F32)], axis=0)
 
     cps = {}
     for m, e in groups:
@@ -361,11 +517,11 @@
         u = u + s2[i]
     share = tally * (1.0 / G)
     a = lax.rsqrt(u[3:6] + FLOOR)
-    b = lax.rsqrt(u[6:9] + FLOOR)
+    b = inv_gmeas
     gcos = u[0:3] * a * b
     wall[me] = jnp.concatenate(
         [share * a * b, share * gcos * a * a,
-         jnp.sum(share * gcos, axis=0, keepdims=True), jnp.zeros((1, GA), F32), u[8:16]], axis=0)
+         jnp.sum(share * gcos, axis=0, keepdims=True), u[6:7]], axis=0)
     cps = []
     for m, e in groups:
         cp = remote(wall.at[me], wall.at[me], s3_s.at[m, e], s3_r.at[m, e], group(m, e))
@@ -407,17 +563,24 @@
         gz[t] = cp
         pending.append(cp)
 
-    top = k.LV - 1
     to_core(0)
     gz[high] = remote(gp.at[0, 0], gp.at[high, 0], gz_s.at[high], gz_r.at[high], group(high, 0))
-    pending.append(gz[high])
+
+    for b in range(top):
+        t = 1 << b
+        gz[t] = remote(gp.at[0, 0], gp.at[t, 0], gz_s.at[t], gz_r.at[t], group(t, 0))
+
+    def near_start():
+        for b in reversed(range(top)):
+            gz[1 << b].start()
 
     @pl.when(c == 0)
     def _():
         gz[high].start()
 
-    for b in reversed(range(top)):
-        to_plane(0, b)
+    @pl.when(c == 1)
+    def _():
+        near_start()
 
     for m, e in groups:
         dcp[m, e].wait_recv()
@@ -438,9 +601,9 @@
     gsum = jnp.sum(gene_total, axis=1, keepdims=True)
     dens = jnp.zeros((1, 1), F32)
     for s in range(SLIDES):
-        dens = dens + tally[s:s + 1] * fin[9:10, 1 + s:2 + s]
+        dens = dens + tally[s:s + 1] * fin[7:8, 1 + s:2 + s]
     lid = lax.broadcasted_iota(jnp.int32, (8, 128), 1)
-    out_loss[...] = (jnp.where(lid == 0, fin[9:10, 0:1], 0.0) + jnp.where(lid == 1, gsum, 0.0)
+    out_loss[...] = (jnp.where(lid == 0, fin[7:8, 0:1], 0.0) + jnp.where(lid == 1, gsum, 0.0)
                      + jnp.where(lid == 2, dens, 0.0)) / total_tally
 
     ycp = {}
@@ -465,6 +628,8 @@
             return 0
 
         lax.fori_loop(0, NC // RC, step, 0)
+
+    def send_map(m, es):
         for e in es:
             src = ybuf.at[pl.ds((m * 2 + e) * X, X)]
             if m == 0 and type(e) is int and e == 0:
@@ -481,6 +646,7 @@
             if (m, e) != (0, 0):
                 i2[m, e].wait_recv()
         map_rows(m, [0, 1], lambda: gp[m].reshape(2 * S, G))
+        send_map(m, [0, 1])
 
     gc[0].wait_recv()
     map_piece(0)
@@ -505,12 +671,16 @@
 
     @pl.when(c == 0)
     def _():
+        gz[high].wait_send()
+        pl.semaphore_signal(gate, inc=1, device_id=group(0, 1), device_id_type=MESH_ID)
+        near_start()
         high_on()
 
     @pl.when(c == 1)
     def _():
+        pl.semaphore_wait(gate, 1)
+        gz[high].start()
         gc[high].wait_recv()
-        gz[high].start()
 
     i2[high, 0].wait_recv()
     i2[high, 1].wait_recv()
@@ -524,7 +694,9 @@
     def _():
         gc[high].wait_recv()
 
+    send_map(high, [c])
     map_rows(high, [1 - c], lambda: gp[high, 1 - c])
+    send_map(high, [1 - c])
     for b in reversed(range(top)):
         for m in range(1 << b, Z, 2 << b):
             gz[m].wait_recv()
@@ -604,7 +776,7 @@
 
     def put_own(half):
         def put(lanes, v):
-            out_single[half * H:(half + 1) * H, lanes] = v
+            own_single[half * H:(half + 1) * H, lanes] = v
         return put
 
     for half in range(2):
@@ -616,21 +788,39 @@
 
         def step(i, _):
             lanes = pl.ds(pl.multiple_of(i * NN, NN), NN)
-            v = out_single[half * H:(half + 1) * H, lanes]
+            v = own_single[half * H:(half + 1) * H, lanes]
             for i2_ in halves[half]:
                 v = v + grecv[i2_, :, lanes].astype(F32)
-            out_single[half * H:(half + 1) * H, lanes] = v * float(k.CELLS) ** 0.5
+            own_single[half * H:(half + 1) * H, lanes] = v * float(k.CELLS) ** 0.5
             return 0
 
         lax.fori_loop(0, G // NN, step, 0)
+
+    cp_single = pltpu.make_async_copy(own_single, out_single, loc_sem.at[4])
+    cp_single.start()
 
     for m, e in groups:
         other = (flip(z, m), slice(None), flip(c, e))
         remote(ybuf.at[pl.ds(0, X)], out_map.at[other[0], :, other[2]], y_s.at[m, e], y_r.at[m, e],
                group(m, e)).wait_recv()
     ycp[0, 0].wait()
+    cp_single.wait()
     for cp in pending:
         cp.wait_send()
+    for b in range(top):
+        gz[1 << b].wait_send()
+
+    @pl.when(c == 1)
+    def _():
+        gz[high].wait_send()
+
+    @pl.when(at_end)
+    def _():
+        sent([high])
+
+    @pl.when(inside)
+    def _():
+        sent(far)
 
 
 def forward_and_back(k, logits, single_cell, spatial, ids, mask, cell_prior, order):
@@ -644,14 +834,13 @@
         pltpu.VMEM((Z, 2, X, YR, S), BF16),
         pltpu.VMEM((NC, G), BF16),
         pltpu.VMEM((NC, A * S), BF16),
-        pltpu.VMEM(((A - 2) * S, NC), BF16),
+        pltpu.VMEM((A * S, NC), BF16),
         pltpu.VMEM((A * X, YR, S), BF16),
         pltpu.VMEM((Z, 2, 8, S), F32),
         pltpu.VMEM((Z, 2, 8, S), F32),
         pltpu.VMEM((Z, S, G), F32),
         pltpu.VMEM((Z, S, G), BF16),
         pltpu.VMEM((Z, S, G), BF16),
-        pltpu.VMEM((Z - 1, S, G), BF16),
         pltpu.VMEM((Z - 1, S, G), BF16),
         pltpu.VMEM((S, G), BF16),
         pltpu.VMEM((Z, 2, S, G), BF16),
@@ -663,12 +852,15 @@
         pltpu.VMEM((16, A * S), BF16),
         pltpu.VMEM((Z, 2, 8, S), F32),
         pltpu.VMEM((Z, 2, 8, S), F32),
-        pltpu.VMEM((A, 16, GA), F32),
-        pltpu.VMEM((Z, 2, 16, GA), F32),
-        pltpu.VMEM((16, GA), F32),
-        pltpu.VMEM((Q - 1, 16, GA), F32),
-        pltpu.VMEM((A, 16, GA), F32),
-        dma(4),
+        pltpu.VMEM((A, 8, GA), F32),
+        pltpu.VMEM((Z, 2, 8, GA), F32),
+        pltpu.VMEM((A, 8, GA), F32),
+        pltpu.VMEM((Z, 2, 8, GA), F32),
+        pltpu.VMEM((8, GA), F32),
+        pltpu.VMEM((Q - 1, 8, GA), F32),
+        pltpu.VMEM((A, 8, GA), F32),
+        pltpu.VMEM((R, G), F32),
+        dma(6),
         dma(Z, 2), dma(Z, 2),
         dma(ncl), dma(ncl),
         dma(Z, 2), dma(Z, 2),
@@ -684,6 +876,8 @@
         dma(Z, 2), dma(Z, 2),
         dma(Z, 2), dma(Z, 2),
         dma(ngs), dma(ngs),
+        dma(Z, 2), dma(Z, 2),
+        pltpu.SemaphoreType.REGULAR,
     ]
     return pl.pallas_call(
         functools.partial(kernel, k),
@@ -694,7 +888,7 @@
             jax.ShapeDtypeStruct((8, 128), F32),
         ],
         in_specs=[hbm, hbm, hbm, vm, vm, vm, vm, vm],
-        out_specs=[hbm, vm, vm],
+        out_specs=[hbm, hbm, vm],
         scratch_shapes=scratch,
         compiler_params=pltpu.CompilerParams(
             collective_id=0, has_side_effects=True, vmem_limit_bytes=64000 * 1024),

time: 293 us -> 278 us (0.949)
  the two profiles are of different devices: /device:TPU:9 before, /device:TPU:0 now
where the time goes in v3:
time: 278 us; the launch traced here: 277 us
  Pallas kernels  268 us (96%)
  other arithmetic  5.41 us (2%)
  local copies, waits for them, and re-layouts  3.21 us (1%)
    pallas_call x1, Pallas kernels, forward_and_back(): pl.pallas_call(functools.partial(kernel, k), name='mapping', out_shape=[j...  268 us

profile of v3, /device:TPU:0, one launch (start us, length us, event | category | flops | bytes accessed | tf_op | source)
XLA Modules:
  0.0 277.4 jit_solution(6232882472488836520)
XLA Ops:
  0.6 268.1 %mapping.1 = (bf16[4,2,2,1024,128]{4,3,2,1,0:T(8,128)(2,1)}, f32[512,2048]{1,0:T(8,128)}, f32[8,128]{1,0:T(8,128)}) custom-call(bf16[4,2,2,1024,128]{4,3,2,1,0:T(8,128)(2,1)} %bitcast.11, bf16[16,1024,128]{2,1,0:T(8,128)(2,1)} %bitcast.12, bf16[512,2048]{1,0:T(8,128)(2,1)} %own_cells.1, bf16[128,2048]{1,0:T(8,128)(2,1)} %spatial.1, s32[1,128]{1,0:T(1,128)} %bitcast.14, ...), custom_call_target="tpu_custom_call" | custom-call | flops 25769803776 | bytes 33554432 | tf_op jit(solution)/shard_map/mapping/pallas_call | solution.py:882
  268.8 1.2 slice_bitcast_fusion
  270.0 0.0 copy-start
  270.0 5.4 %bitcast_convert_fusion = f32[16384,128]{1,0:T(8,128)} fusion(bf16[4,2,2,1024,128]{4,3,2,1,0:T(8,128)(2,1)} %get-tuple-element.7), kind=kLoop, calls=%fused_computation | loop fusion | flops 2097152 | bytes 12582912 | tf_op jit(solution)/shard_map/convert_element_type | solution.py:906
  275.4 0.0 copy-done
  275.4 2.0 copy.11
Async XLA Ops:
  270.0 5.4 %copy-start = (f32[512,2048]{1,0:T(8,128)S(1)}, f32[512,2048]{1,0:T(8,128)}, u32[]{:S(2)}) copy-start(f32[512,2048]{1,0:T(8,128)} %get-tuple-element.14) | copy-start | bytes 12582916

commit v4 on v3

--- a/solution.py
+++ b/solution.py
@@ -351,7 +351,7 @@
 
     @pl.when(inside & (c == 0))
     def _():
-        send_logits(far)
+        send_logits(far, (1, 0))
 
     @pl.when(at_end)
     def _():
@@ -378,7 +378,9 @@
         for m in of_level(b, near):
             predict_pair(m)
         send_level(b, of_level(b, near))
-    predict_pair(0)
+    @pl.when(at_end)
+    def _():
+        predict_pair(0)
 
     @pl.when(inside)
     def _():
@@ -393,6 +395,7 @@
             cross_shares(m, 0)
             predict_cross(m, 0)
         far_levels(0)
+        predict_pair(0)
 
         @pl.when(c == 0)
         def _():
@@ -629,17 +632,22 @@
 
         lax.fori_loop(0, NC // RC, step, 0)
 
-    def send_map(m, es):
+    def map_copies(m, es):
+        cps = []
         for e in es:
             src = ybuf.at[pl.ds((m * 2 + e) * X, X)]
             if m == 0 and type(e) is int and e == 0:
-                cp = pltpu.make_async_copy(src, out_map.at[z, :, c], loc_sem.at[3])
-                cp.start()
-                ycp[0, 0] = cp
+                cps.append(pltpu.make_async_copy(src, out_map.at[z, :, c], loc_sem.at[3]))
+                ycp[0, 0] = cps[-1]
             else:
-                cp = remote(src, out_map.at[z, :, c], y_s.at[m, e], y_r.at[m, e], group(m, e))
-                cp.start()
-                pending.append(cp)
+                cps.append(remote(src, out_map.at[z, :, c], y_s.at[m, e], y_r.at[m, e],
+                                  group(m, e)))
+                pending.append(cps[-1])
+        return cps
+
+    def send_map(m, es):
+        for cp in map_copies(m, es):
+            cp.start()
 
     def map_piece(m):
         for e in range(2):
@@ -694,16 +702,23 @@
     def _():
         gc[high].wait_recv()
 
-    send_map(high, [c])
+    own_core = map_copies(high, [c])
+
+    @pl.when(at_end)
+    def _():
+        own_core[0].start()
+
     map_rows(high, [1 - c], lambda: gp[high, 1 - c])
+
+    @pl.when(inside)
+    def _():
+        own_core[0].start()
+
     send_map(high, [1 - c])
     for b in reversed(range(top)):
         for m in range(1 << b, Z, 2 << b):
             gz[m].wait_recv()
             pass_on(m, b)
-    for m in far + near:
-        gc[m].wait_recv()
-
     def slot_of(dx, dy, half):
         return ((dx * Y + dy) - 1) * 2 + half
 
@@ -712,13 +727,14 @@
         by = flip(y, dy)
         return pl.multiple_of(((bx * Y + by) * 2 + half) * H, H)
 
-    def single_part(dx, dy, half, put):
+    def single_part(dx, dy, half, put, m0=0, m1=Z):
         r0 = single_rows(dx, dy, half)
+        n = (m1 - m0) * 2 * S
 
         def step(i, _):
             lanes = pl.ds(pl.multiple_of(i * NN, NN), NN)
-            v = jnp.dot(slow[pl.ds(r0, H), :], gp[:, :, :, lanes].reshape(A * S, NN),
-                        preferred_element_type=F32)
+            v = jnp.dot(slow[pl.ds(r0, H), m0 * 2 * S:m1 * 2 * S],
+                        gp[pl.ds(m0, m1 - m0), :, :, lanes].reshape(n, NN), preferred_element_type=F32)
             put(lanes, v)
             return 0
 
@@ -731,6 +747,17 @@
             gsend[slot, :, lanes] = v.astype(BF16)
         return put
 
+    def put_own(half):
+        def put(lanes, v):
+            own_single[half * H:(half + 1) * H, lanes] = v
+        return put
+
+    def put_rest(sl, half):
+        def put(lanes, v):
+            v = v + own_single[half * H:(half + 1) * H, lanes]
+            gsend[sl, :, lanes] = v.astype(BF16)
+        return put
+
     r_m1 = lambda d: d
     r_m2 = lambda d: XN + d
     r_m3 = lambda d: 2 * XN + d
@@ -744,12 +771,24 @@
         gcp[r_slot] = cp
         pending.append(cp)
 
+    for m in range(1, Z - 1):
+        if m != high:
+            gc[m].wait_recv()
+    for half in range(2):
+        single_part(1, 1, half, put_own(half), 0, Z - 1)
+    if Z > 2:
+        gc[Z - 1].wait_recv()
     for d in range(XN):
-        s0, s1_ = slot_of(d + 1, 1, 0), slot_of(d + 1, 1, 1)
-        single_part(d + 1, 1, 0, put_send(s0))
-        send_single(s0, r_m1(d), plane(d + 1, 0))
-        single_part(d + 1, 1, 1, put_send(s1_))
-        send_single(s1_, r_m2(d), plane(0, 1))
+        for half in range(2):
+            sl = slot_of(d + 1, 1, half)
+            if d == 0:
+                single_part(1, 1, half, put_rest(sl, half), Z - 1, Z)
+            else:
+                single_part(d + 1, 1, half, put_send(sl))
+            if half == 0:
+                send_single(sl, r_m1(d), plane(d + 1, 0))
+            else:
+                send_single(sl, r_m2(d), plane(0, 1))
     for m in far:
         map_piece(m)
     for d in range(XN):
@@ -774,13 +813,9 @@
     single_part(0, 1, 0, put_send(s0, [r_m1(d) for d in range(XN)]))
     send_single(s0, r_m6, plane(0, 1))
 
-    def put_own(half):
-        def put(lanes, v):
-            own_single[half * H:(half + 1) * H, lanes] = v
-        return put
-
     for half in range(2):
         single_part(0, 0, half, put_own(half))
+    cp_single = []
     halves = [[r_m3(d) for d in range(XN)] + [r_m6], [r_m5(d) for d in range(XN)] + [r_m4]]
     for half in range(2):
         for i in halves[half]:
@@ -795,16 +830,18 @@
             return 0
 
         lax.fori_loop(0, G // NN, step, 0)
-
-    cp_single = pltpu.make_async_copy(own_single, out_single, loc_sem.at[4])
-    cp_single.start()
+        rows_h = pl.ds(half * H, H)
+        cp_single.append(pltpu.make_async_copy(
+            own_single.at[rows_h], out_single.at[rows_h], loc_sem.at[4 + half]))
+        cp_single[half].start()
 
     for m, e in groups:
         other = (flip(z, m), slice(None), flip(c, e))
         remote(ybuf.at[pl.ds(0, X)], out_map.at[other[0], :, other[2]], y_s.at[m, e], y_r.at[m, e],
                group(m, e)).wait_recv()
     ycp[0, 0].wait()
-    cp_single.wait()
+    for cp in cp_single:
+        cp.wait()
     for cp in pending:
         cp.wait_send()
     for b in range(top):

time: 278 us -> 275 us (0.989)
  the two profiles are of different devices: /device:TPU:0 before, /device:TPU:9 now
where the time goes in v4:
time: 275 us
  Pallas kernels  265 us (96%)
  other arithmetic  5.41 us (2%)
  local copies, waits for them, and re-layouts  3.21 us (1%)
    pallas_call x1, Pallas kernels, forward_and_back(): pl.pallas_call(functools.partial(kernel, k), name='mapping', out_shape=[j...  265 us

profile of v4, /device:TPU:9, one launch (start us, length us, event | category | flops | bytes accessed | tf_op | source)
XLA Modules:
  0.0 274.7 jit_solution(4298876280129384902)
XLA Ops:
  0.6 265.4 %mapping.1 = (bf16[4,2,2,1024,128]{4,3,2,1,0:T(8,128)(2,1)}, f32[512,2048]{1,0:T(8,128)}, f32[8,128]{1,0:T(8,128)}) custom-call(bf16[4,2,2,1024,128]{4,3,2,1,0:T(8,128)(2,1)} %bitcast.11, bf16[16,1024,128]{2,1,0:T(8,128)(2,1)} %bitcast.12, bf16[512,2048]{1,0:T(8,128)(2,1)} %own_cells.1, bf16[128,2048]{1,0:T(8,128)(2,1)} %spatial.1, s32[1,128]{1,0:T(1,128)} %bitcast.14, ...), custom_call_target="tpu_custom_call" | custom-call | flops 25769803776 | bytes 33554432 | tf_op jit(solution)/shard_map/mapping/pallas_call | solution.py:919
  266.1 1.2 slice_bitcast_fusion
  267.3 0.0 copy-start
  267.3 5.4 %bitcast_convert_fusion = f32[16384,128]{1,0:T(8,128)} fusion(bf16[4,2,2,1024,128]{4,3,2,1,0:T(8,128)(2,1)} %get-tuple-element.7), kind=kLoop, calls=%fused_computation | loop fusion | flops 2097152 | bytes 12582912 | tf_op jit(solution)/shard_map/convert_element_type | solution.py:943
  272.7 0.0 copy-done
  272.7 2.0 copy.11
Async XLA Ops:
  267.3 5.4 %copy-start = (f32[512,2048]{1,0:T(8,128)S(1)}, f32[512,2048]{1,0:T(8,128)}, u32[]{:S(2)}) copy-start(f32[512,2048]{1,0:T(8,128)} %get-tuple-element.14) | copy-start | bytes 12582916

commit v5 on v4

--- a/solution.py
+++ b/solution.py
@@ -8,6 +8,7 @@
 from jax.sharding import Mesh, PartitionSpec as P
 
 SLIDES = 3
+HALVES = 2
 FLOOR = 1e-06
 F32 = jnp.float32
 BF16 = jnp.bfloat16
@@ -72,8 +73,8 @@
             src_ref=src, dst_ref=dst, send_sem=send, recv_sem=recv,
             device_id=where, device_id_type=MESH_ID)
 
-    groups = [(m, e) for m in range(Z) for e in range(2) if (m, e) != (0, 0)]
-    planes = [(dx, dy) for dx in range(X) for dy in range(Y) if (dx, dy) != (0, 0)]
+    groups = [(m, e) for m in reversed(range(Z)) for e in (1, 0) if (m, e) != (0, 0)]
+    planes = [(dx, dy) for dx in reversed(range(X)) for dy in (1, 0) if (dx, dy) != (0, 0)]
     me = z * 2 + c
     pending = []
 
@@ -248,15 +249,36 @@
     def cross_shares(m, cc):
         make_shares(m, slot(cc), t_row(m, cc))
 
-    ps = [remote(p1.at[m], psib.at[m], ps_s.at[m], ps_r.at[m], group(0, 1)) for m in range(Z)]
+    gene_part = [pl.ds(h * (G // HALVES), G // HALVES) for h in range(HALVES)]
+
+    class Parts:
+        def __init__(self, make):
+            self.cps = [make(h) for h in range(HALVES)]
+
+        def start(self):
+            for cp in self.cps:
+                cp.start()
+
+        def wait_send(self):
+            for cp in self.cps:
+                cp.wait_send()
+
+    def sibling_part(m):
+        return Parts(lambda h: remote(
+            p1.at[m, :, gene_part[h]], psib.at[m, :, gene_part[h]], ps_s.at[m, h], ps_r.at[m, h],
+            group(0, 1)))
+
+    ps = [sibling_part(m) for m in range(Z)]
     pending.extend(ps)
 
-    def gene_loop(put):
+    def gene_loop(put, h=0, parts=1):
+        n = G // NN // parts
+
         def step(i, _):
             put(pl.ds(pl.multiple_of(i * NN, NN), NN))
             return 0
 
-        lax.fori_loop(0, G // NN, step, 0)
+        lax.fori_loop(h * n, (h + 1) * n, step, 0)
 
     def predict_pair(m):
         row = t_row(m, 0)
@@ -287,25 +309,26 @@
             def put(lanes):
                 p1[m, :, lanes] = part(lanes).astype(BF16)
 
-            gene_loop(put)
-            ps[m].start()
+            for h in range(HALVES):
+                gene_loop(put, h, HALVES)
+                ps[m].cps[h].start()
 
     def level_slot(b, m):
         return sum(Z >> (j + 1) for j in range(b)) + (m >> (b + 1))
 
-    rs = {}
-    for b in range(k.LV):
-        step_m = 1 << b
-        for m in range(0, Z, 2 * step_m):
-            sl = level_slot(b, m)
-            rs[b, m] = remote(psib.at[m ^ step_m], rs_in.at[sl], rs_s.at[sl], rs_r.at[sl],
-                              group(step_m, 0))
+    def level_part(b, m):
+        sl, step_m = level_slot(b, m), 1 << b
+        return Parts(lambda h: remote(
+            psib.at[m ^ step_m, :, gene_part[h]], rs_in.at[sl, :, gene_part[h]],
+            rs_s.at[sl, h], rs_r.at[sl, h], group(step_m, 0)))
+
+    rs = {(b, m): level_part(b, m) for b in range(k.LV) for m in range(0, Z, 2 << b)}
     pending.extend(rs.values())
 
-    def piece_sum(m, b):
-        ps[m].wait_recv()
+    def piece_sum(m, b, h):
+        ps[m].cps[h].wait_recv()
         for j in range(b):
-            rs[j, m].wait_recv()
+            rs[j, m].cps[h].wait_recv()
 
         def total(lanes):
             t = pacc[m, :, lanes] + psib[m, :, lanes].astype(F32)
@@ -314,11 +337,16 @@
             return t
         return total
 
-    def sum_level(b, m):
-        total = piece_sum(m, b)
-        for j in range(A):
-            lanes = slice(j * GA, (j + 1) * GA)
-            psib[m, :, lanes] = total(lanes).astype(BF16)
+    per_part = A // HALVES
+
+    def sum_level(b, m, send=True):
+        for h in range(HALVES):
+            total = piece_sum(m, b, h)
+            for j in range(h * per_part, (h + 1) * per_part):
+                lanes = slice(j * GA, (j + 1) * GA)
+                psib[m, :, lanes] = total(lanes).astype(BF16)
+            if send:
+                rs[b, m ^ (1 << b)].cps[h].start()
 
     def far_levels(cc):
         @pl.when(c == cc)
@@ -329,7 +357,6 @@
     def send_level(b, ms):
         for m in ms:
             sum_level(b, m)
-            rs[b, m ^ (1 << b)].start()
 
     top = k.LV - 1
     def of_level(b, ms):
@@ -399,23 +426,24 @@
 
         @pl.when(c == 0)
         def _():
-            sum_level(top, high)
+            sum_level(top, high, False)
 
         for m in far:
             wait_cross(m, 1)
-            cross_shares(m, 1)
-            predict_cross(m, 1)
 
         @pl.when(c == 0)
         def _():
             rs[top, 0].start()
 
+        for m in far:
+            cross_shares(m, 1)
+            predict_cross(m, 1)
+
         far_levels(1)
 
     @pl.when(at_end | (c == 1))
     def _():
         sum_level(top, high)
-        rs[top, 0].start()
 
     mem_rows = jnp.concatenate(
         [info[m, e, 1:1 + SLIDES, :] for m in range(Z) for e in range(2)], axis=1)
@@ -473,12 +501,13 @@
         dcp[m, e] = cp
         pending.append(cp)
 
-    total = piece_sum(0, k.LV)
     pred_sq = jnp.zeros((S, 1), F32)
     pred_meas = jnp.zeros((S, 1), F32)
     lane_id = lax.broadcasted_iota(jnp.int32, (1, GA), 1)
     for j in range(A):
         lanes = slice(j * GA, (j + 1) * GA)
+        if j % per_part == 0:
+            total = piece_sum(0, k.LV, j // per_part)
         p = total(lanes)
         pacc[0, :, lanes] = p
         q = meas[:, lanes].astype(F32)
@@ -901,8 +930,8 @@
         dma(Z, 2), dma(Z, 2),
         dma(ncl), dma(ncl),
         dma(Z, 2), dma(Z, 2),
-        dma(Z), dma(Z),
-        dma(Z - 1), dma(Z - 1),
+        dma(Z, HALVES), dma(Z, HALVES),
+        dma(Z - 1, HALVES), dma(Z - 1, HALVES),
         dma(Q - 1), dma(Q - 1),
         dma(Z, 2), dma(Z, 2),
         dma(Z, 2), dma(Z, 2),

time: 275 us -> 272 us (0.989)
    pallas_call x1, Pallas kernels: 265 us -> 263 us  [forward_and_back(): pl.pallas_call(functools.partial(kernel, k), name='mapping', out_shape=[j...]
where the time goes in v5:
time: 272 us
  Pallas kernels  263 us (97%)
  other arithmetic  5.41 us (2%)
  local copies, waits for them, and re-layouts  3.21 us (1%)
    pallas_call x1, Pallas kernels, forward_and_back(): pl.pallas_call(functools.partial(kernel, k), name='mapping', out_shape=[j...  263 us

profile of v5, /device:TPU:9, one launch (start us, length us, event | category | flops | bytes accessed | tf_op | source)
XLA Modules:
  0.0 271.8 jit_solution(10037476592520482706)
XLA Ops:
  0.6 262.5 %mapping.1 = (bf16[4,2,2,1024,128]{4,3,2,1,0:T(8,128)(2,1)}, f32[512,2048]{1,0:T(8,128)}, f32[8,128]{1,0:T(8,128)}) custom-call(bf16[4,2,2,1024,128]{4,3,2,1,0:T(8,128)(2,1)} %bitcast.11, bf16[16,1024,128]{2,1,0:T(8,128)(2,1)} %bitcast.12, bf16[512,2048]{1,0:T(8,128)(2,1)} %own_cells.1, bf16[128,2048]{1,0:T(8,128)(2,1)} %spatial.1, s32[1,128]{1,0:T(1,128)} %bitcast.14, ...), custom_call_target="tpu_custom_call" | custom-call | flops 25769803776 | bytes 33554432 | tf_op jit(solution)/shard_map/mapping/pallas_call | solution.py:948
  263.2 1.2 slice_bitcast_fusion
  264.3 0.0 copy-start
  264.4 5.4 %bitcast_convert_fusion = f32[16384,128]{1,0:T(8,128)} fusion(bf16[4,2,2,1024,128]{4,3,2,1,0:T(8,128)(2,1)} %get-tuple-element.7), kind=kLoop, calls=%fused_computation | loop fusion | flops 2097152 | bytes 12582912 | tf_op jit(solution)/shard_map/convert_element_type | solution.py:972
  269.8 0.0 copy-done
  269.8 2.0 copy.11
Async XLA Ops:
  264.3 5.4 %copy-start = (f32[512,2048]{1,0:T(8,128)S(1)}, f32[512,2048]{1,0:T(8,128)}, u32[]{:S(2)}) copy-start(f32[512,2048]{1,0:T(8,128)} %get-tuple-element.14) | copy-start | bytes 12582916

commit v6 on v5

--- a/solution.py
+++ b/solution.py
@@ -44,6 +44,7 @@
         self.GA = genes // self.A
         self.RC = min(256, self.YR)
         self.PL = min(128, self.YR)
+        self.PLANE = 2 * self.Q == self.A
         self.NN = min(512, genes)
 
 
@@ -53,10 +54,10 @@
            pacc, p1, psib, rs_in, meas,
            gp, gsend, grecv,
            mass_out, mass_in, ratio_hl, mext, dpart, din,
-           mstat, mstat_in, stat, s1, ubuf, s2, wall, own_single,
+           mstat, mstat_in, gm_out, gm_in, stat, s1, ubuf, s2, wall, own_single,
            loc_sem, lg_s, lg_r, cl_s, cl_r, in_s, in_r, ps_s, ps_r, rs_s, rs_r, ms_s, ms_r,
            d_s, d_r, s1_s, s1_r, s2_s, s2_r, s3_s, s3_r, gz_s, gz_r, gc_s, gc_r, i2_s, i2_r,
-           y_s, y_r, gs_s, gs_r, mt_s, mt_r, gate):
+           y_s, y_r, gs_s, gs_r, mt_s, mt_r, gate, gm_s, gm_r):
     Z, X, Y, A, Q, S, G, R, H = k.Z, k.X, k.Y, k.A, k.Q, k.S, k.G, k.R, k.H
     YR, NC, GA, RC, NN = k.YR, k.NC, k.GA, k.RC, k.NN
     z, x, c, y = [lax.axis_index(a) for a in AXES]
@@ -76,6 +77,28 @@
     groups = [(m, e) for m in reversed(range(Z)) for e in (1, 0) if (m, e) != (0, 0)]
     planes = [(dx, dy) for dx in reversed(range(X)) for dy in (1, 0) if (dx, dy) != (0, 0)]
     me = z * 2 + c
+
+    def part_of(dx, dy, e):
+        return (lax.rem(x + dx, X) * Y + flip(y, dy)) * 2 + c + e - 2 * c * e
+
+    if k.PLANE:
+        mine = part_of(0, 0, 0)
+        sharers = [(dx * Y + dy, e, part_of(dx, dy, e),
+                    (z, lax.rem(x + dx, X), c + e - 2 * c * e, flip(y, dy)))
+                   for dx in reversed(range(X)) for dy in (1, 0) for e in (1, 0)
+                   if (dx, dy, e) != (0, 0, 0)]
+        others = [(m - 1, group(m, 0)) for m in reversed(range(1, Z))]
+    else:
+        mine = me
+        sharers = [(m, e, flip(z, m) * 2 + flip(c, e), group(m, e)) for m, e in groups]
+        others = [(i, plane(dx, dy)) for i, (dx, dy) in enumerate(planes)]
+
+    def tree_sum(first, parts):
+        v = [first] + list(parts)
+        while len(v) > 1:
+            v = [v[i] + v[i + 1] if i + 1 < len(v) else v[i] for i in range(0, len(v), 2)]
+        return v[0]
+
     pending = []
 
     cp_flat = pltpu.make_async_copy(logits_flat, ybuf, loc_sem.at[0])
@@ -90,7 +113,13 @@
         pl.semaphore_signal(barrier, inc=1, device_id=group(m, e), device_id_type=MESH_ID)
     for dx, dy in planes:
         pl.semaphore_signal(barrier, inc=1, device_id=plane(dx, dy), device_id_type=MESH_ID)
-    pl.semaphore_wait(barrier, len(groups) + len(planes))
+    greeted = len(groups) + len(planes)
+    if k.PLANE:
+        for dx, dy in planes:
+            pl.semaphore_signal(barrier, inc=1, device_id=(*plane(dx, dy)[:2], 1 - c, flip(y, dy)),
+                                device_id_type=MESH_ID)
+        greeted += len(planes)
+    pl.semaphore_wait(barrier, greeted)
 
     def rows(bx, by, half):
         return cells.at[pl.ds(pl.multiple_of(((bx * Y + by) * 2 + half) * H, H), H)]
@@ -180,10 +209,9 @@
         mstat[j, SLIDES:8, :] = jnp.zeros((8 - SLIDES, GA), F32)
     inv_meas = lax.rsqrt(meas_sq + FLOOR)
     mst = {}
-    for m, e in groups:
-        mst[m, e] = remote(mstat.at[flip(z, m) * 2 + flip(c, e)], mstat_in.at[m, e],
-                           mt_s.at[m, e], mt_r.at[m, e], group(m, e))
-        mst[m, e].start()
+    for i, e, part, where in sharers:
+        mst[i, e] = remote(mstat.at[part], mstat_in.at[i, e], mt_s.at[i, e], mt_r.at[i, e], where)
+        mst[i, e].start()
     pending.extend(mst.values())
 
     fwd_a, fwd_b = [], []
@@ -448,16 +476,23 @@
     mem_rows = jnp.concatenate(
         [info[m, e, 1:1 + SLIDES, :] for m in range(Z) for e in range(2)], axis=1)
     mem16 = jnp.concatenate([mem_rows, jnp.zeros((16 - SLIDES, A * S), F32)], axis=0).astype(BF16)
-    part = lax.dot_general(mem16, slow[...], (((1,), (1,)), ((), ())), preferred_element_type=F32)
+    part_mass = lax.dot_general(mem16, slow[...], (((1,), (1,)), ((), ())), preferred_element_type=F32)
     col_tally = jnp.sum(mem_rows, axis=1, keepdims=True)
-    gmeas = mstat[me]
-    for m, e in groups:
-        mst[m, e].wait_recv()
-        gmeas = gmeas + mstat_in[m, e]
+    gmeas = mstat[mine]
+    for i, e, part, where in sharers:
+        mst[i, e].wait_recv()
+        gmeas = gmeas + mstat_in[i, e]
     packed = [gmeas[s:s + 1] for s in range(SLIDES)] + [jnp.zeros((1, NC - SLIDES * GA), F32)]
     mass_out[...] = jnp.concatenate(
-        [part[:SLIDES], jnp.broadcast_to(col_tally, (SLIDES, NC)),
+        [part_mass[:SLIDES], jnp.broadcast_to(col_tally, (SLIDES, NC)),
          jnp.concatenate(packed, axis=1), jnp.zeros((1, NC), F32)], axis=0)
+    gmc = []
+    if k.PLANE:
+        gm_out[...] = gmeas
+        for i, where in others:
+            gmc.append(remote(gm_out, gm_in.at[i], gm_s.at[i], gm_r.at[i], where))
+            gmc[-1].start()
+        pending.extend(gmc)
     mcp = []
     for i, (dx, dy) in enumerate(planes):
         cp = remote(mass_out, mass_in.at[i], ms_s.at[i], ms_r.at[i], plane(dx, dy))
@@ -526,43 +561,44 @@
     for j in range(A):
         stat[j, 6:8, :] = jnp.concatenate([scal, jnp.zeros((1, GA), F32)], axis=0)
 
-    cps = {}
-    for m, e in groups:
-        cp = remote(stat.at[flip(z, m) * 2 + flip(c, e)], s1.at[m, e],
-                    s1_s.at[m, e], s1_r.at[m, e], group(m, e))
-        cp.start()
-        cps[m, e] = cp
-        pending.append(cp)
-    u = stat[me]
-    for m, e in groups:
-        cps[m, e].wait_recv()
-        u = u + s1[m, e]
+    cps = []
+    for i, e, part, where in sharers:
+        cp = remote(stat.at[part], s1.at[i, e], s1_s.at[i, e], s1_r.at[i, e], where)
+        cp.start()
+        cps.append(cp)
+    pending.extend(cps)
+    u = stat[mine]
+    for (i, e, part, where), cp in zip(sharers, cps):
+        cp.wait_recv()
+        u = u + s1[i, e]
     ubuf[...] = u
     cps = []
-    for i, (dx, dy) in enumerate(planes):
-        cp = remote(ubuf, s2.at[i], s2_s.at[i], s2_r.at[i], plane(dx, dy))
+    for i, where in others:
+        cp = remote(ubuf, s2.at[i], s2_s.at[i], s2_r.at[i], where)
         cp.start()
         cps.append(cp)
-        pending.append(cp)
-    for i, cp in enumerate(cps):
+    pending.extend(cps)
+    for cp in cps + gmc:
         cp.wait_recv()
-        u = u + s2[i]
+    u = tree_sum(u, [s2[i] for i in range(len(others))])
+    if k.PLANE:
+        gmeas = tree_sum(gm_out[...], [gm_in[i] for i in range(len(others))])[:SLIDES]
+        inv_gmeas = lax.rsqrt(gmeas + FLOOR)
     share = tally * (1.0 / G)
     a = lax.rsqrt(u[3:6] + FLOOR)
     b = inv_gmeas
     gcos = u[0:3] * a * b
-    wall[me] = jnp.concatenate(
+    wall[mine] = jnp.concatenate(
         [share * a * b, share * gcos * a * a,
          jnp.sum(share * gcos, axis=0, keepdims=True), u[6:7]], axis=0)
     cps = []
-    for m, e in groups:
-        cp = remote(wall.at[me], wall.at[me], s3_s.at[m, e], s3_r.at[m, e], group(m, e))
+    for i, e, part, where in sharers:
+        cp = remote(wall.at[mine], wall.at[mine], s3_s.at[i, e], s3_r.at[i, e], where)
         cp.start()
         cps.append(cp)
-        pending.append(cp)
-    for (m, e) in groups:
-        other = flip(z, m) * 2 + flip(c, e)
-        remote(wall.at[other], wall.at[other], s3_s.at[m, e], s3_r.at[m, e], group(m, e)).wait_recv()
+    pending.extend(cps)
+    for i, e, part, where in sharers:
+        remote(wall.at[part], wall.at[part], s3_s.at[i, e], s3_r.at[i, e], where).wait_recv()
 
     lead = -(wcol * inv_pred * inv_meas)
     back = wcol * spot_cos * inv_pred * inv_pred
@@ -920,6 +956,8 @@
         pltpu.VMEM((Z, 2, 8, S), F32),
         pltpu.VMEM((A, 8, GA), F32),
         pltpu.VMEM((Z, 2, 8, GA), F32),
+        pltpu.VMEM((8, GA), F32),
+        pltpu.VMEM((Q - 1, 8, GA), F32),
         pltpu.VMEM((A, 8, GA), F32),
         pltpu.VMEM((Z, 2, 8, GA), F32),
         pltpu.VMEM((8, GA), F32),
@@ -944,6 +982,7 @@
         dma(ngs), dma(ngs),
         dma(Z, 2), dma(Z, 2),
         pltpu.SemaphoreType.REGULAR,
+        dma(Q - 1), dma(Q - 1),
     ]
     return pl.pallas_call(
         functools.partial(kernel, k),

time: 272 us -> 272 us (level)
  no operation moved by 1% of the time
where the time goes in v6:
time: 272 us; the launch traced here: 271 us
  Pallas kernels  262 us (96%)
  other arithmetic  5.41 us (2%)
  local copies, waits for them, and re-layouts  3.21 us (1%)
    pallas_call x1, Pallas kernels, forward_and_back(): pl.pallas_call(functools.partial(kernel, k), name='mapping', out_shape=[j...  262 us

profile of v6, /device:TPU:9, one launch (start us, length us, event | category | flops | bytes accessed | tf_op | source)
XLA Modules:
  0.0 271.4 jit_solution(11702292912728167234)
XLA Ops:
  0.6 262.1 %mapping.1 = (bf16[4,2,2,1024,128]{4,3,2,1,0:T(8,128)(2,1)}, f32[512,2048]{1,0:T(8,128)}, f32[8,128]{1,0:T(8,128)}) custom-call(bf16[4,2,2,1024,128]{4,3,2,1,0:T(8,128)(2,1)} %bitcast.11, bf16[16,1024,128]{2,1,0:T(8,128)(2,1)} %bitcast.12, bf16[512,2048]{1,0:T(8,128)(2,1)} %own_cells.1, bf16[128,2048]{1,0:T(8,128)(2,1)} %spatial.1, s32[1,128]{1,0:T(1,128)} %bitcast.14, ...), custom_call_target="tpu_custom_call" | custom-call | flops 25769803776 | bytes 33554432 | tf_op jit(solution)/shard_map/mapping/pallas_call | solution.py:987
  262.8 1.2 slice_bitcast_fusion
  264.0 0.0 copy-start
  264.0 5.4 %bitcast_convert_fusion = f32[16384,128]{1,0:T(8,128)} fusion(bf16[4,2,2,1024,128]{4,3,2,1,0:T(8,128)(2,1)} %get-tuple-element.7), kind=kLoop, calls=%fused_computation | loop fusion | flops 2097152 | bytes 12582912 | tf_op jit(solution)/shard_map/convert_element_type | solution.py:1011
  269.4 0.0 copy-done
  269.4 2.0 copy.11
Async XLA Ops:
  264.0 5.4 %copy-start = (f32[512,2048]{1,0:T(8,128)S(1)}, f32[512,2048]{1,0:T(8,128)}, u32[]{:S(2)}) copy-start(f32[512,2048]{1,0:T(8,128)} %get-tuple-element.14) | copy-start | bytes 12582916

commit v7 on v6

--- a/solution.py
+++ b/solution.py
@@ -458,14 +458,12 @@
 
         for m in far:
             wait_cross(m, 1)
+            cross_shares(m, 1)
+            predict_cross(m, 1)
 
         @pl.when(c == 0)
         def _():
             rs[top, 0].start()
-
-        for m in far:
-            cross_shares(m, 1)
-            predict_cross(m, 1)
 
         far_levels(1)
 

time: 272 us -> 271 us (level)
  no operation moved by 1% of the time
where the time goes in v7:
time: 271 us
  Pallas kernels  261 us (96%)
  other arithmetic  5.41 us (2%)
  local copies, waits for them, and re-layouts  3.21 us (1%)
    pallas_call x1, Pallas kernels, forward_and_back(): pl.pallas_call(functools.partial(kernel, k), name='mapping', out_shape=[j...  261 us

profile of v7, /device:TPU:9, one launch (start us, length us, event | category | flops | bytes accessed | tf_op | source)
XLA Modules:
  0.0 270.6 jit_solution(18301661549911790251)
XLA Ops:
  0.6 261.3 %mapping.1 = (bf16[4,2,2,1024,128]{4,3,2,1,0:T(8,128)(2,1)}, f32[512,2048]{1,0:T(8,128)}, f32[8,128]{1,0:T(8,128)}) custom-call(bf16[4,2,2,1024,128]{4,3,2,1,0:T(8,128)(2,1)} %bitcast.11, bf16[16,1024,128]{2,1,0:T(8,128)(2,1)} %bitcast.12, bf16[512,2048]{1,0:T(8,128)(2,1)} %own_cells.1, bf16[128,2048]{1,0:T(8,128)(2,1)} %spatial.1, s32[1,128]{1,0:T(1,128)} %bitcast.14, ...), custom_call_target="tpu_custom_call" | custom-call | flops 25769803776 | bytes 33554432 | tf_op jit(solution)/shard_map/mapping/pallas_call | solution.py:985
  262.0 1.2 slice_bitcast_fusion
  263.1 0.0 copy-start
  263.1 5.4 %bitcast_convert_fusion = f32[16384,128]{1,0:T(8,128)} fusion(bf16[4,2,2,1024,128]{4,3,2,1,0:T(8,128)(2,1)} %get-tuple-element.7), kind=kLoop, calls=%fused_computation | loop fusion | flops 2097152 | bytes 12582912 | tf_op jit(solution)/shard_map/convert_element_type | solution.py:1009
  268.6 0.0 copy-done
  268.6 2.0 copy.11
Async XLA Ops:
  263.1 5.4 %copy-start = (f32[512,2048]{1,0:T(8,128)S(1)}, f32[512,2048]{1,0:T(8,128)}, u32[]{:S(2)}) copy-start(f32[512,2048]{1,0:T(8,128)} %get-tuple-element.14) | copy-start | bytes 12582916

commit v8 on v7

--- a/solution.py
+++ b/solution.py
@@ -42,7 +42,7 @@
         self.YR = self.Y * self.R
         self.NC = self.X * self.YR
         self.GA = genes // self.A
-        self.RC = min(256, self.YR)
+        self.RC = min(512, self.YR)
         self.PL = min(128, self.YR)
         self.PLANE = 2 * self.Q == self.A
         self.NN = min(512, genes)

time: 271 us -> 270 us (level)
  no operation moved by 1% of the time
where the time goes in v8:
time: 270 us; the launch traced here: 269 us
  Pallas kernels  260 us (96%)
  other arithmetic  5.41 us (2%)
  local copies, waits for them, and re-layouts  3.21 us (1%)
    pallas_call x1, Pallas kernels, forward_and_back(): pl.pallas_call(functools.partial(kernel, k), name='mapping', out_shape=[j...  260 us
    convert_element_type x1, other arithmetic, body(): grad_map = gmap.reshape(cells, spots).astype(F32)  5.41 us

profile of v8, /device:TPU:9, one launch (start us, length us, event | category | flops | bytes accessed | tf_op | source)
XLA Modules:
  0.0 269.4 jit_solution(581915392456040988)
XLA Ops:
  0.6 260.1 %mapping.1 = (bf16[4,2,2,1024,128]{4,3,2,1,0:T(8,128)(2,1)}, f32[512,2048]{1,0:T(8,128)}, f32[8,128]{1,0:T(8,128)}) custom-call(bf16[4,2,2,1024,128]{4,3,2,1,0:T(8,128)(2,1)} %bitcast.11, bf16[16,1024,128]{2,1,0:T(8,128)(2,1)} %bitcast.12, bf16[512,2048]{1,0:T(8,128)(2,1)} %own_cells.1, bf16[128,2048]{1,0:T(8,128)(2,1)} %spatial.1, s32[1,128]{1,0:T(1,128)} %bitcast.14, ...), custom_call_target="tpu_custom_call" | custom-call | flops 25769803776 | bytes 33554432 | tf_op jit(solution)/shard_map/mapping/pallas_call | solution.py:985
  260.8 1.2 slice_bitcast_fusion
  262.0 0.0 copy-start
  262.0 5.4 %bitcast_convert_fusion = f32[16384,128]{1,0:T(8,128)} fusion(bf16[4,2,2,1024,128]{4,3,2,1,0:T(8,128)(2,1)} %get-tuple-element.7), kind=kLoop, calls=%fused_computation | loop fusion | flops 2097152 | bytes 12582912 | tf_op jit(solution)/shard_map/convert_element_type | solution.py:1009
  267.4 0.0 copy-done
  267.4 2.0 copy.11
Async XLA Ops:
  262.0 5.4 %copy-start = (f32[512,2048]{1,0:T(8,128)S(1)}, f32[512,2048]{1,0:T(8,128)}, u32[]{:S(2)}) copy-start(f32[512,2048]{1,0:T(8,128)} %get-tuple-element.14) | copy-start | bytes 12582916
